TPU v7x, 128 devices: a whole 4x4x4 slice. The times are simulated.
128 devices in a mesh: seq: 8 (over z, core), dp: 16 (over y, x).
Axes of the slice: x: 4, y: 4, z: 4, core: 2. Of those that a mesh axis runs over, the one named last changes fastest.
Arguments:
- inputs: bfloat16 [16, 1024, 768], P('dp', 'seq'), may hold values from -6 to 6
- doc_ids: int32 [16, 1024], P('dp', 'seq'), may hold values from 0 to 4, as said below
- cotangent: bfloat16 [16, 1024, 768], P('dp', 'seq'), may hold values from -6 to 6
- w_query: float32 [768, 768], P(('seq', 'dp')), may hold values from -0.21875 to 0.21875
- w_key: float32 [768, 768], P(('seq', 'dp')), may hold values from -0.21875 to 0.21875
- w_value: float32 [768, 768], P(('seq', 'dp')), may hold values from -0.21875 to 0.21875
- w_output: float32 [768, 768], P(('seq', 'dp')), may hold values from -3.5 to 3.5
- w_gate: float32 [768, 3072], P(('seq', 'dp')), may hold values from -0.21875 to 0.21875
- w_up: float32 [768, 3072], P(('seq', 'dp')), may hold values from -0.21875 to 0.21875
- w_down: float32 [3072, 768], P(('seq', 'dp')), may hold values from -0.109375 to 0.109375
- norm_gains: float32 [768, 2], P(('seq', 'dp')), may hold values from 0.5 to 1.5
- mom_query: float32 [768, 768], P(('seq', 'dp')), may hold values from -80 to 80
- mom_key: float32 [768, 768], P(('seq', 'dp')), may hold values from -80 to 80
- mom_value: float32 [768, 768], P(('seq', 'dp')), may hold values from -80 to 80
- mom_output: float32 [768, 768], P(('seq', 'dp')), may hold values from -3.5 to 3.5
- mom_gate: float32 [768, 3072], P(('seq', 'dp')), may hold values from -40 to 40
- mom_up: float32 [768, 3072], P(('seq', 'dp')), may hold values from -40 to 40
- mom_down: float32 [3072, 768], P(('seq', 'dp')), may hold values from -40 to 40
- mom_gains: float32 [768, 2], P(('seq', 'dp')), may hold values from -80 to 80
- avg_query: float32 [768, 768], P(('seq', 'dp')), may hold values from -0.21875 to 0.21875
- avg_key: float32 [768, 768], P(('seq', 'dp')), may hold values from -0.21875 to 0.21875
- avg_value: float32 [768, 768], P(('seq', 'dp')), may hold values from -0.21875 to 0.21875
- avg_output: float32 [768, 768], P(('seq', 'dp')), may hold values from -3.5 to 3.5
- avg_gate: float32 [768, 3072], P(('seq', 'dp')), may hold values from -0.21875 to 0.21875
- avg_up: float32 [768, 3072], P(('seq', 'dp')), may hold values from -0.21875 to 0.21875
- avg_down: float32 [3072, 768], P(('seq', 'dp')), may hold values from -0.109375 to 0.109375
- avg_gains: float32 [768, 2], P(('seq', 'dp')), may hold values from 0.5 to 1.5
Outputs:
- output: bfloat16 [16, 1024, 768], P('dp', 'seq')
- input_grad: float32 [16, 1024, 768], P('dp', 'seq')
- new_query: float32 [768, 768], P(('seq', 'dp'))
- new_key: float32 [768, 768], P(('seq', 'dp'))
- new_value: float32 [768, 768], P(('seq', 'dp'))
- new_output: float32 [768, 768], P(('seq', 'dp'))
- new_gate: float32 [768, 3072], P(('seq', 'dp'))
- new_up: float32 [768, 3072], P(('seq', 'dp'))
- new_down: float32 [3072, 768], P(('seq', 'dp'))
- new_gains: float32 [768, 2], P(('seq', 'dp'))
- moment_query: float32 [768, 768], P(('seq', 'dp'))
- moment_key: float32 [768, 768], P(('seq', 'dp'))
- moment_value: float32 [768, 768], P(('seq', 'dp'))
- moment_output: float32 [768, 768], P(('seq', 'dp'))
- moment_gate: float32 [768, 3072], P(('seq', 'dp'))
- moment_up: float32 [768, 3072], P(('seq', 'dp'))
- moment_down: float32 [3072, 768], P(('seq', 'dp'))
- moment_gains: float32 [768, 2], P(('seq', 'dp'))
- mean_query: float32 [768, 768], P(('seq', 'dp'))
- mean_key: float32 [768, 768], P(('seq', 'dp'))
- mean_value: float32 [768, 768], P(('seq', 'dp'))
- mean_output: float32 [768, 768], P(('seq', 'dp'))
- mean_gate: float32 [768, 3072], P(('seq', 'dp'))
- mean_up: float32 [768, 3072], P(('seq', 'dp'))
- mean_down: float32 [3072, 768], P(('seq', 'dp'))
- mean_gains: float32 [768, 2], P(('seq', 'dp'))
- copy_query: bfloat16 [768, 768], P(('seq', 'dp'))
- copy_key: bfloat16 [768, 768], P(('seq', 'dp'))
- copy_value: bfloat16 [768, 768], P(('seq', 'dp'))
- copy_output: bfloat16 [768, 768], P(('seq', 'dp'))
- copy_gate: bfloat16 [768, 3072], P(('seq', 'dp'))
- copy_up: bfloat16 [768, 3072], P(('seq', 'dp'))
- copy_down: bfloat16 [3072, 768], P(('seq', 'dp'))
- copy_gains: bfloat16 [768, 2], P(('seq', 'dp'))
Inputs may be any that keep to these rules, and one draw needn't show every extreme that they name: `doc_ids`: ids never fall along a sequence and start at 0; in every sequence one document begins within the first device's block of 128 tokens and ends within the last one's.
All inputs are finite; a program needn't handle non-finite values.
Results may differ from a plain program's by a relative error of at most 0.02.
Values may be sent and summed in bfloat16 or wider, within the bound.
No kernel may reach another device: no remote copies, remote signals or barrier semaphores. Data moves between devices by JAX's collectives and lax.ppermute only.
A program may use at most 192 MiB of HBM per device.

v0:
```python
import math

import jax
import jax.numpy as jnp
from jax import lax
from jax.sharding import PartitionSpec as P

H = 12
KV = 12
HD = 64


EPS = 1e-05
MOMENTUM = 0.9
AVERAGE = 0.5
RATES = (0.01, 0.01, 0.01, 4.0, 0.02, 0.02, 0.015, 0.1)
MASKED = -1e30


def turn_angles(places):
    freq = 10000.0 ** (-jnp.arange(0, HD, 2, dtype=jnp.float32) / HD)
    theta = places.astype(jnp.float32)[:, None] * freq[None, :]
    theta = jnp.concatenate([theta, theta], axis=-1)
    return (jnp.cos(theta), jnp.sin(theta))


def rotate(vecs, cosine, sine):
    half = vecs.shape[-1] // 2
    turned = jnp.concatenate([-vecs[..., half:], vecs[..., :half]], axis=-1)
    return vecs * cosine[:, None, :] + turned * sine[:, None, :]


def rotate_back(grads, cosine, sine):
    half = grads.shape[-1] // 2
    moved = grads * sine[:, None, :]
    turned = jnp.concatenate([moved[..., half:], -moved[..., :half]], axis=-1)
    return grads * cosine[:, None, :] + turned


def norm_forward(values, gain):
    scale = lax.rsqrt(jnp.mean(values * values, axis=-1, keepdims=True) + EPS)
    return (values * scale * gain, scale)


def norm_backward(values, gain, scale, grad):
    weighted = grad * gain
    gain_grad = jnp.sum(grad * values * scale, axis=0)
    inner = jnp.mean(weighted * values, axis=-1, keepdims=True)
    return (scale * weighted - values * scale**3 * inner, gain_grad)


def masked_scores(qblock, keys, ids_block, idx_block, key_ids, factor):
    scores = jnp.einsum("qkgd,skd->kgqs", qblock, keys, preferred_element_type=jnp.float32) * factor
    key_index = jnp.arange(keys.shape[0], dtype=jnp.int32)
    allowed = (ids_block[:, None] == key_ids[None, :]) & (key_index[None, :] <= idx_block[:, None])
    return jnp.where(allowed[None, None], scores, MASKED)


def attend_forward(queries, keys, values, ids_parts, idx_parts, key_ids, factor):

    def one(item):
        qblock, ids_block, idx_block = item
        scores = masked_scores(qblock, keys, ids_block, idx_block, key_ids, factor)
        top = jnp.max(scores, axis=-1, keepdims=True)
        expo = jnp.exp(scores - top)
        total = jnp.sum(expo, axis=-1, keepdims=True)
        probs = (expo / total).astype(jnp.bfloat16)
        mixed = jnp.einsum("kgqs,skd->qkgd", probs, values, preferred_element_type=jnp.float32)
        return (mixed.astype(jnp.bfloat16), top + jnp.log(total))

    return lax.map(one, (queries, ids_parts, idx_parts))


def attend_backward(queries, keys, values, grads_out, lse, ids_parts, idx_parts, key_ids, factor):

    def one(carry, item):
        key_acc, value_acc = carry
        qblock, gblock, lblock, ids_block, idx_block = item
        scores = masked_scores(qblock, keys, ids_block, idx_block, key_ids, factor)
        probs = jnp.exp(scores - lblock)
        dprob = jnp.einsum("qkgd,skd->kgqs", gblock, values, preferred_element_type=jnp.float32)
        inner = jnp.sum(dprob * probs, axis=-1, keepdims=True)
        dscore = (probs * (dprob - inner)).astype(jnp.bfloat16)
        dquery = (
            jnp.einsum("kgqs,skd->qkgd", dscore, keys, preferred_element_type=jnp.float32) * factor
        )
        key_acc = (
            key_acc
            + jnp.einsum("kgqs,qkgd->skd", dscore, qblock, preferred_element_type=jnp.float32)
            * factor
        )
        value_acc = value_acc + jnp.einsum(
            "kgqs,qkgd->skd", probs.astype(jnp.bfloat16), gblock, preferred_element_type=jnp.float32
        )
        return ((key_acc, value_acc), dquery)

    zeros = jnp.zeros(keys.shape, jnp.float32)
    return lax.scan(one, (zeros, zeros), (queries, grads_out, lse, ids_parts, idx_parts))


def update(master, moment, average, grad, rate):
    moment_new = MOMENTUM * moment + grad
    weight_new = master - rate * (grad + MOMENTUM * moment_new)
    mean_new = AVERAGE * average + (1.0 - AVERAGE) * weight_new
    return (weight_new, moment_new, mean_new, weight_new.astype(jnp.bfloat16))


def shards(
    inputs,
    doc_ids,
    cotangent,
    w_query,
    w_key,
    w_value,
    w_output,
    w_gate,
    w_up,
    w_down,
    norm_gains,
    mom_query,
    mom_key,
    mom_value,
    mom_output,
    mom_gate,
    mom_up,
    mom_down,
    mom_gains,
    avg_query,
    avg_key,
    avg_value,
    avg_output,
    avg_gate,
    avg_up,
    avg_down,
    avg_gains,
):
    bf = jnp.bfloat16
    f32 = jnp.float32
    wq, wk, wv, wo, wg, wu, wd, gain_pair = (
        lax.all_gather(w_query.astype(bf), ("seq", "dp"), axis=0, tiled=True),
        lax.all_gather(w_key.astype(bf), ("seq", "dp"), axis=0, tiled=True),
        lax.all_gather(w_value.astype(bf), ("seq", "dp"), axis=0, tiled=True),
        lax.all_gather(w_output.astype(bf), ("seq", "dp"), axis=0, tiled=True),
        lax.all_gather(w_gate.astype(bf), ("seq", "dp"), axis=0, tiled=True),
        lax.all_gather(w_up.astype(bf), ("seq", "dp"), axis=0, tiled=True),
        lax.all_gather(w_down.astype(bf), ("seq", "dp"), axis=0, tiled=True),
        lax.all_gather(norm_gains.astype(bf), ("seq", "dp"), axis=0, tiled=True),
    )
    x = inputs[0].astype(f32)
    span = x.shape[0]
    group = H // KV
    kv_width = KV * HD
    factor = HD ** (-0.5)
    ids_all = lax.all_gather(doc_ids, "seq", axis=1, tiled=True)[0]
    length = ids_all.shape[0]
    own_ids = doc_ids[0]
    own_index = lax.axis_index("seq") * span + jnp.arange(span, dtype=jnp.int32)
    starts = jnp.sum((ids_all[None, :] < own_ids[:, None]).astype(jnp.int32), axis=1)
    cosine, sine = turn_angles(own_index - starts)
    block = max(1, min(span, 131072 // length))
    while span % block:
        block -= 1
    count = span // block
    ids_parts = own_ids.reshape(count, block)
    idx_parts = own_index.reshape(count, block)
    gain_one = gain_pair[:, 0].astype(f32)
    gain_two = gain_pair[:, 1].astype(f32)
    normed_one, scale_one = norm_forward(x, gain_one)
    h1 = normed_one.astype(bf)
    q32 = jnp.dot(h1, wq, preferred_element_type=f32).reshape(span, H, HD)
    k32 = jnp.dot(h1, wk, preferred_element_type=f32).reshape(span, KV, HD)
    v16 = jnp.dot(h1, wv, preferred_element_type=f32).astype(bf)
    q16 = rotate(q32, cosine, sine).astype(bf).reshape(count, block, KV, group, HD)
    k16 = rotate(k32, cosine, sine).astype(bf).reshape(span, kv_width)
    keys, values = (
        lax.all_gather(k16, "seq", axis=0, tiled=True),
        lax.all_gather(v16, "seq", axis=0, tiled=True),
    )
    keys = keys.reshape(length, KV, HD)
    values = values.reshape(length, KV, HD)
    mixed, lse = attend_forward(q16, keys, values, ids_parts, idx_parts, ids_all, factor)
    attn16 = mixed.reshape(span, H * HD)
    resid = x + jnp.dot(attn16, wo, preferred_element_type=f32)
    normed_two, scale_two = norm_forward(resid, gain_two)
    h2 = normed_two.astype(bf)
    gate = jnp.dot(h2, wg, preferred_element_type=f32)
    up = jnp.dot(h2, wu, preferred_element_type=f32)
    sig = jax.nn.sigmoid(gate)
    hidden = (gate * sig * up).astype(bf)
    output = (resid + jnp.dot(hidden, wd, preferred_element_type=f32)).astype(bf)
    wq, wk, wv, wo, wg, wu, wd, gain_pair = (
        lax.all_gather(w_query.astype(bf), ("seq", "dp"), axis=0, tiled=True),
        lax.all_gather(w_key.astype(bf), ("seq", "dp"), axis=0, tiled=True),
        lax.all_gather(w_value.astype(bf), ("seq", "dp"), axis=0, tiled=True),
        lax.all_gather(w_output.astype(bf), ("seq", "dp"), axis=0, tiled=True),
        lax.all_gather(w_gate.astype(bf), ("seq", "dp"), axis=0, tiled=True),
        lax.all_gather(w_up.astype(bf), ("seq", "dp"), axis=0, tiled=True),
        lax.all_gather(w_down.astype(bf), ("seq", "dp"), axis=0, tiled=True),
        lax.all_gather(norm_gains.astype(bf), ("seq", "dp"), axis=0, tiled=True),
    )
    dy = cotangent[0]
    dhid = jnp.einsum("cd,fd->cf", dy, wd, preferred_element_type=f32)
    dgate = (dhid * up * sig * (1.0 + gate * (1.0 - sig))).astype(bf)
    dup = (dhid * gate * sig).astype(bf)
    dh2 = jnp.einsum("cf,df->cd", dgate, wg, preferred_element_type=f32)
    dh2 = dh2 + jnp.einsum("cf,df->cd", dup, wu, preferred_element_type=f32)
    dres_norm, grad_two = norm_backward(resid, gain_two, scale_two, dh2)
    dres = dy.astype(f32) + dres_norm
    grad_down = jnp.einsum("cf,cd->fd", hidden, dy, preferred_element_type=f32)
    grad_gate = jnp.einsum("cd,cf->df", h2, dgate, preferred_element_type=f32)
    grad_up = jnp.einsum("cd,cf->df", h2, dup, preferred_element_type=f32)
    sum_gate, sum_up, sum_down, sum_two = (
        lax.psum_scatter(grad_gate, ("seq", "dp"), scatter_dimension=0, tiled=True),
        lax.psum_scatter(grad_up, ("seq", "dp"), scatter_dimension=0, tiled=True),
        lax.psum_scatter(grad_down, ("seq", "dp"), scatter_dimension=0, tiled=True),
        lax.psum_scatter(grad_two[:, None], ("seq", "dp"), scatter_dimension=0, tiled=True),
    )
    dres16 = dres.astype(bf)
    dattn = jnp.einsum("cd,ad->ca", dres16, wo, preferred_element_type=f32).astype(bf)
    dattn = dattn.reshape(count, block, KV, group, HD)
    (key_acc, value_acc), dquery = attend_backward(
        q16, keys, values, dattn, lse, ids_parts, idx_parts, ids_all, factor
    )
    term = jnp.concatenate(
        [key_acc.reshape(length, kv_width), value_acc.reshape(length, kv_width)], axis=1
    )
    kv_sum = lax.psum_scatter(
        term.astype(jnp.bfloat16), "seq", scatter_dimension=0, tiled=True
    ).astype(jnp.float32)
    dq16 = rotate_back(dquery.reshape(span, H, HD), cosine, sine).astype(bf).reshape(span, H * HD)
    dk16 = (
        rotate_back(kv_sum[:, :kv_width].reshape(span, KV, HD), cosine, sine)
        .astype(bf)
        .reshape(span, kv_width)
    )
    dv16 = kv_sum[:, kv_width:].astype(bf)
    dh1 = jnp.einsum("ca,da->cd", dq16, wq, preferred_element_type=f32)
    dh1 = dh1 + jnp.einsum("ca,da->cd", dk16, wk, preferred_element_type=f32)
    dh1 = dh1 + jnp.einsum("ca,da->cd", dv16, wv, preferred_element_type=f32)
    dx_norm, grad_one = norm_backward(x, gain_one, scale_one, dh1)
    input_grad = dres + dx_norm
    grad_out = jnp.einsum("ca,cd->ad", attn16, dres16, preferred_element_type=f32)
    grad_query = jnp.einsum("cd,ca->da", h1, dq16, preferred_element_type=f32)
    grad_key = jnp.einsum("cd,ca->da", h1, dk16, preferred_element_type=f32)
    grad_value = jnp.einsum("cd,ca->da", h1, dv16, preferred_element_type=f32)
    sum_query, sum_key, sum_value, sum_out, sum_one = (
        lax.psum_scatter(grad_query, ("seq", "dp"), scatter_dimension=0, tiled=True),
        lax.psum_scatter(grad_key, ("seq", "dp"), scatter_dimension=0, tiled=True),
        lax.psum_scatter(grad_value, ("seq", "dp"), scatter_dimension=0, tiled=True),
        lax.psum_scatter(grad_out, ("seq", "dp"), scatter_dimension=0, tiled=True),
        lax.psum_scatter(grad_one[:, None], ("seq", "dp"), scatter_dimension=0, tiled=True),
    )
    sum_gains = jnp.concatenate([sum_one, sum_two], axis=1)
    tokens_all = inputs.shape[0] * span * lax.axis_size("seq") * lax.axis_size("dp")
    base = 1.0 / math.sqrt(tokens_all)
    masters = (w_query, w_key, w_value, w_output, w_gate, w_up, w_down, norm_gains)
    moments = (mom_query, mom_key, mom_value, mom_output, mom_gate, mom_up, mom_down, mom_gains)
    averages = (avg_query, avg_key, avg_value, avg_output, avg_gate, avg_up, avg_down, avg_gains)
    sums = (sum_query, sum_key, sum_value, sum_out, sum_gate, sum_up, sum_down, sum_gains)
    done = [update(masters[i], moments[i], averages[i], sums[i], RATES[i] * base) for i in range(8)]
    news = [item[0] for item in done]
    moms = [item[1] for item in done]
    means = [item[2] for item in done]
    copies = [item[3] for item in done]
    return (
        output[None],
        input_grad[None],
        news[0],
        news[1],
        news[2],
        news[3],
        news[4],
        news[5],
        news[6],
        news[7],
        moms[0],
        moms[1],
        moms[2],
        moms[3],
        moms[4],
        moms[5],
        moms[6],
        moms[7],
        means[0],
        means[1],
        means[2],
        means[3],
        means[4],
        means[5],
        means[6],
        means[7],
        copies[0],
        copies[1],
        copies[2],
        copies[3],
        copies[4],
        copies[5],
        copies[6],
        copies[7],
    )


def solution(mesh):
    return jax.shard_map(
        shards,
        mesh=mesh,
        in_specs=(
            P("dp", "seq", None),
            P("dp", "seq"),
            P("dp", "seq", None),
            P(("seq", "dp"), None),
            P(("seq", "dp"), None),
            P(("seq", "dp"), None),
            P(("seq", "dp"), None),
            P(("seq", "dp"), None),
            P(("seq", "dp"), None),
            P(("seq", "dp"), None),
            P(("seq", "dp"), None),
            P(("seq", "dp"), None),
            P(("seq", "dp"), None),
            P(("seq", "dp"), None),
            P(("seq", "dp"), None),
            P(("seq", "dp"), None),
            P(("seq", "dp"), None),
            P(("seq", "dp"), None),
            P(("seq", "dp"), None),
            P(("seq", "dp"), None),
            P(("seq", "dp"), None),
            P(("seq", "dp"), None),
            P(("seq", "dp"), None),
            P(("seq", "dp"), None),
            P(("seq", "dp"), None),
            P(("seq", "dp"), None),
            P(("seq", "dp"), None),
        ),
        out_specs=(
            P("dp", "seq", None),
            P("dp", "seq", None),
            P(("seq", "dp"), None),
            P(("seq", "dp"), None),
            P(("seq", "dp"), None),
            P(("seq", "dp"), None),
            P(("seq", "dp"), None),
            P(("seq", "dp"), None),
            P(("seq", "dp"), None),
            P(("seq", "dp"), None),
            P(("seq", "dp"), None),
            P(("seq", "dp"), None),
            P(("seq", "dp"), None),
            P(("seq", "dp"), None),
            P(("seq", "dp"), None),
            P(("seq", "dp"), None),
            P(("seq", "dp"), None),
            P(("seq", "dp"), None),
            P(("seq", "dp"), None),
            P(("seq", "dp"), None),
            P(("seq", "dp"), None),
            P(("seq", "dp"), None),
            P(("seq", "dp"), None),
            P(("seq", "dp"), None),
            P(("seq", "dp"), None),
            P(("seq", "dp"), None),
            P(("seq", "dp"), None),
            P(("seq", "dp"), None),
            P(("seq", "dp"), None),
            P(("seq", "dp"), None),
            P(("seq", "dp"), None),
            P(("seq", "dp"), None),
            P(("seq", "dp"), None),
            P(("seq", "dp"), None),
        ),
        check_vma=False,
    )
```

profile of v0, /device:TPU:1, one launch (start us, length us, event | category | flops | bytes accessed | tf_op | source)
XLA Modules:
  0.0 1870.9 jit_solution(3164152992002898502)
XLA Ops:
  13.7 52.3 %all-gather = bf16[128,6,2]{1,2,0:T(2,128)(2,1)S(1)} all-gather(bf16[1,6,2]{1,2,0:T(2,128)(2,1)S(1)} %convert_bitcast_fusion.7), channel_id=1, replica_groups=mesh['seq'=8,'dp'=16] {'seq','dp'}, dimensions={0}, use_global_device_ids=true | all-gather | bytes 3096 | tf_op jit(solution)/shard_map/all_gather | solution.py:147
  67.7 11.6 all-gather.23.cloned.1.call-done
  82.8 8.7 all_gather.45
  91.9 52.5 %all-gather.25.cloned.1.call-done = bf16[128,6,768]{2,1,0:T(8,128)(2,1)} async-done(((bf16[1,6,768]{2,1,0:T(8,128)(2,1)}), bf16[128,6,768]{2,1,0:T(8,128)(2,1)}) %all-gather.25.cloned.1.call-update) | async-done | bytes 1179664 | tf_op jit(solution)/shard_map/all_gather | solution.py:141
  148.1 61.2 %all-gather.27.cloned.1.call-done = bf16[128,6,768]{2,1,0:T(8,128)(2,1)} async-done(((bf16[1,6,768]{2,1,0:T(8,128)(2,1)}), bf16[128,6,768]{2,1,0:T(8,128)(2,1)}) %all-gather.27.cloned.1.call-update) | async-done | bytes 1179664 | tf_op jit(solution)/shard_map/all_gather | solution.py:140
  220.4 53.8 %all-gather.29.cloned.1.call-done = bf16[128,6,768]{2,1,0:T(8,128)(2,1)} async-done(((bf16[1,6,768]{2,1,0:T(8,128)(2,1)}), bf16[128,6,768]{2,1,0:T(8,128)(2,1)}) %all-gather.29.cloned.1.call-update) | async-done | bytes 1179664 | tf_op jit(solution)/shard_map/all_gather | solution.py:143
  276.5 21.8 %all-gather.17.cloned.1.call-done = bf16[1024,768]{1,0:T(8,128)(2,1)} async-done(((bf16[128,768]{1,0:T(8,128)(2,1)}), bf16[1024,768]{1,0:T(8,128)(2,1)}) %all-gather.17.cloned.1.call-update) | async-done | bytes 1572880 | tf_op jit(solution)/shard_map/all_gather | solution.py:177
  300.0 25.8 %all-gather.19.cloned.1.call-done = bf16[1024,768]{0,1:T(8,128)(2,1)} async-done(((bf16[128,768]{0,1:T(8,128)(2,1)}), bf16[1024,768]{0,1:T(8,128)(2,1)}) %all-gather.19.cloned.1.call-update) | async-done | bytes 1572880 | tf_op jit(solution)/shard_map/all_gather | solution.py:176
  333.3 65.2 %all-gather.31.cloned.1.call-done = bf16[128,6,3072]{2,1,0:T(8,128)(2,1)} async-done(((bf16[1,6,3072]{2,1,0:T(8,128)(2,1)}), bf16[128,6,3072]{2,1,0:T(8,128)(2,1)}) %all-gather.31.cloned.1.call-update) | async-done | bytes 4718608 | tf_op jit(solution)/shard_map/all_gather | solution.py:144
  398.5 7.8 reshape.433
  406.3 61.7 %all-gather.33.cloned.1.call-done = bf16[128,6,3072]{2,1,0:T(8,128)(2,1)} async-done(((bf16[1,6,3072]{2,1,0:T(8,128)(2,1)}), bf16[128,6,3072]{2,1,0:T(8,128)(2,1)}) %all-gather.33.cloned.1.call-update) | async-done | bytes 4718608 | tf_op jit(solution)/shard_map/all_gather | solution.py:145
  467.9 8.2 reshape.435
  482.0 54.0 %all-gather.21.cloned.1.call-done = bf16[3072,768]{1,0:T(8,128)(2,1)} async-done(((bf16[24,768]{1,0:T(8,128)(2,1)}), bf16[3072,768]{1,0:T(8,128)(2,1)}) %all-gather.21.cloned.1.call-update) | async-done | bytes 4718608 | tf_op jit(solution)/shard_map/all_gather | solution.py:146
  536.0 5.5 multiply_convert_fusion.1
  584.3 10.8 reduce-scatter.21.cloned.1.call-done
  606.2 461.2 %fusion.81 = (f32[8,768]{1,0:T(8,128)S(1)}, f32[8,768]{1,0:T(8,128)S(1)}, f32[8,768]{1,0:T(8,128)S(1)}, f32[8,768]{1,0:T(8,128)}, f32[8,3072]{1,0:T(8,128)S(1)}, /*index=5*/f32[8,3072]{1,0:T(8,128)S(1)}) fusion(f32[768,768]{1,0:T(8,128)} %fusion.62, f32[768,768]{1,0:T(8,128)} %fusion.78, f32[768,768]{1,0:T(8,128)} %fusion.65, f32[768,768]{1,0:T(8,128)} %fusion.67, ...), kind=kCustom, calls=%all-reduce-scatter.6 | all-reduce-scatter fusion | flops 9437185 | bytes 28606464
  1077.5 10.8 collective-permute-start.27
  1088.4 10.3 collective-permute-start.26
  1098.7 24.4 %collective-permute-start.25 = (f32[8,768]{1,0:T(8,128)S(1)}, f32[8,768]{1,0:T(8,128)S(1)}, u32[]{:S(2)}, u32[]{:S(2)}) collective-permute-start(f32[8,768]{1,0:T(8,128)S(1)} %get-tuple-element.111), channel_id=1, source_target_pairs={{0,26},{1,27},{2,28},{3,29},{4,30},{5,31},{6,32},{7,33},{8,34},{9,... | collective-permute-start | bytes 73736
  1132.5 5.9 collective-permute-start.18
  1424.3 64.5 %all-reduce.14 = (f32[768,1]{0,1:T(1,128)S(1)}, f32[768,1]{0,1:T(1,128)S(1)}) all-reduce(f32[768,1]{0,1:T(1,128)S(1)} %broadcast_in_dim.94, f32[768,1]{0,1:T(1,128)S(1)} %broadcast_in_dim.93), channel_id=11, replica_groups=mesh['seq'=8,'dp'=16] {'seq','dp'}, use_global_device_ids=true, to_apply=%region_19.20.clone | all-reduce | flops 1536 | bytes 12288
  1496.2 5.8 collective-permute-start.154
  1528.8 6.7 collective-permute-start.142
  1550.1 23.5 %concatenate.43 = f32[262,768]{1,0:T(8,128)S(1)} concatenate(f32[6,768]{1,0:T(8,128)S(1)} %copy-done.125, f32[8,768]{1,0:T(8,128)S(1)} %copy-done.119, f32[8,768]{1,0:T(8,128)S(1)} %copy-done.121, f32[8,768]{1,0:T(8,128)S(1)} %copy-done.123, f32[8,768]{1,0:T(8,128)S(1)} %copy-done.127, f32[8,768]{1,0:T(8,128)} %copy-done.128, f32[8,768]{1,0:T(8,128)} %copy-done.129, ...), dimensions={0} | concatenate | bytes 1609728
  1589.5 22.0 %concatenate.44 = f32[262,768]{1,0:T(8,128)S(1)} concatenate(f32[6,768]{1,0:T(8,128)S(1)} %copy-done.117, f32[8,768]{1,0:T(8,128)S(1)} %copy-done.149, f32[8,768]{1,0:T(8,128)S(1)} %copy-done.152, f32[8,768]{1,0:T(8,128)S(1)} %copy-done.155, f32[8,768]{1,0:T(8,128)S(1)} %copy-done.158, f32[8,768]{1,0:T(8,128)S(1)} %copy-done.161, f32[8,768]{1,0:T(8,128)S(1)} %copy-done.164, ...), dimensions={0} | concatenate | bytes 1609728
  1613.5 5.6 collective-permute-start.130
  1627.1 27.2 %concatenate.45 = f32[262,768]{1,0:T(8,128)S(1)} concatenate(f32[6,768]{1,0:T(8,128)} %copy-done.115, f32[8,768]{1,0:T(8,128)} %collective-permute-done.94, f32[8,768]{1,0:T(8,128)} %collective-permute-done.93, f32[8,768]{1,0:T(8,128)} %collective-permute-done.92, f32[8,768]{1,0:T(8,128)} %collective-permute-done.91, f32[8,768]{1,0:T(8,128)} %collective-permute-done.90, ...), dimensions={0} | concatenate | bytes 1609728
  1667.2 27.2 %concatenate.46 = f32[262,768]{1,0:T(8,128)S(1)} concatenate(f32[6,768]{1,0:T(8,128)} %copy-done.114, f32[8,768]{1,0:T(8,128)} %collective-permute-done.126, f32[8,768]{1,0:T(8,128)} %collective-permute-done.125, f32[8,768]{1,0:T(8,128)} %collective-permute-done.124, f32[8,768]{1,0:T(8,128)} %collective-permute-done.123, f32[8,768]{1,0:T(8,128)} %collective-permute-done.122, ...), dimensions={0} | concatenate | bytes 1609728
  1709.5 5.4 collective-permute-start.177
  1721.3 5.6 collective-permute-start.174
  1765.9 32.4 %concatenate.47 = f32[262,3072]{1,0:T(8,128)S(1)} concatenate(f32[6,3072]{1,0:T(8,128)} %copy-done.63, f32[8,3072]{1,0:T(8,128)S(1)} %copy-done.61, f32[8,3072]{1,0:T(8,128)} %copy-done.62, f32[8,3072]{1,0:T(8,128)} %copy-done.64, f32[8,3072]{1,0:T(8,128)} %copy-done.65, f32[8,3072]{1,0:T(8,128)} %copy-done.66, f32[8,3072]{1,0:T(8,128)} %copy-done.67, f32[8,3072]{1,0:T(8,128)} %copy-done.68, ...), dimensions={0} | concatenate | bytes 6438912
  1798.3 56.0 %concatenate.48 = f32[262,3072]{1,0:T(8,128)} concatenate(f32[6,3072]{1,0:T(8,128)} %copy-done.59, f32[8,3072]{1,0:T(8,128)} %collective-permute-done.190, f32[8,3072]{1,0:T(8,128)} %collective-permute-done.189, f32[8,3072]{1,0:T(8,128)} %collective-permute-done.188, f32[8,3072]{1,0:T(8,128)} %collective-permute-done.187, f32[8,3072]{1,0:T(8,128)} %collective-permute-done.186, ...), dimensions={0} | concatenate | bytes 6438912
  (903 shorter events, 555.8 us)
Async XLA Ops:
  7.2 72.1 %all-gather.23.cloned.1.call-start = ((), (), s32[]{:S(2)}) async-start(), calls=%async_computation.6 | async-start | bytes 1585152 | tf_op jit(solution)/shard_map/all_gather | solution.py:142
  8.7 135.6 %all-gather.25.cloned.1.call-start = ((), (), s32[]{:S(2)}) async-start(), calls=%async_computation.7 | async-start | bytes 1585152 | tf_op jit(solution)/shard_map/all_gather | solution.py:141
  10.1 199.2 %all-gather.27.cloned.1.call-start = ((), (), s32[]{:S(2)}) async-start(), calls=%async_computation.8 | async-start | bytes 1585152 | tf_op jit(solution)/shard_map/all_gather | solution.py:140
  11.5 262.7 %all-gather.29.cloned.1.call-start = ((), (), s32[]{:S(2)}) async-start(), calls=%async_computation.9 | async-start | bytes 1585152 | tf_op jit(solution)/shard_map/all_gather | solution.py:143
  12.9 285.4 %all-gather.17.cloned.1.call-start = ((), (), s32[]{:S(2)}) async-start(), calls=%async_computation.2 | async-start | bytes 1769472 | tf_op jit(solution)/shard_map/all_gather | solution.py:177
  82.7 243.2 %all-gather.19.cloned.1.call-start = ((), (), s32[]{:S(2)}) async-start(), calls=%async_computation.3 | async-start | bytes 1769472 | tf_op jit(solution)/shard_map/all_gather | solution.py:176
  217.8 180.7 %all-gather.31.cloned.1.call-start = ((), (), s32[]{:S(2)}) async-start(), calls=%async_computation.10 | async-start | bytes 6340608 | tf_op jit(solution)/shard_map/all_gather | solution.py:144
  218.6 249.3 %all-gather.33.cloned.1.call-start = ((), (), s32[]{:S(2)}) async-start(), calls=%async_computation.11 | async-start | bytes 6340608 | tf_op jit(solution)/shard_map/all_gather | solution.py:145
  219.3 316.7 %all-gather.21.cloned.1.call-start = ((), (), s32[]{:S(2)}) async-start(), calls=%async_computation.4 | async-start | bytes 4755456 | tf_op jit(solution)/shard_map/all_gather | solution.py:146
  220.1 375.0 %reduce-scatter.21.cloned.1.call-start = ((), (), s32[]{:S(2)}) async-start(), calls=%async_computation.12 | async-start | bytes 3538944
  565.2 1295.6 %reduce-scatter.19.cloned.1.call-start = ((), (), s32[]{:S(2)}) async-start(), calls=%async_computation.5 | async-start | bytes 9510912 | tf_op jit(solution)/shard_map/reduce_scatter | solution.py:215
  1072.2 50.8 %collective-permute-start.29 = (f32[8,768]{1,0:T(8,128)S(1)}, f32[8,768]{1,0:T(8,128)S(1)}, u32[]{:S(2)}, u32[]{:S(2)}) collective-permute-start(f32[8,768]{1,0:T(8,128)S(1)} %get-tuple-element.111), channel_id=1, source_target_pairs={{0,30},{1,31},{2,32},{3,33},{4,34},{5,35},{6,36},{7,37},{8,38},{9,... | collective-permute-start | bytes 73736
  1073.5 51.6 %collective-permute-start.28 = (f32[8,768]{1,0:T(8,128)S(1)}, f32[8,768]{1,0:T(8,128)S(1)}, u32[]{:S(2)}, u32[]{:S(2)}) collective-permute-start(f32[8,768]{1,0:T(8,128)S(1)} %get-tuple-element.111), channel_id=1, source_target_pairs={{0,29},{1,30},{2,31},{3,32},{4,33},{5,34},{6,35},{7,36},{8,37},{9,... | collective-permute-start | bytes 73736
  1077.5 49.5 %collective-permute-start.27 = (f32[8,768]{1,0:T(8,128)S(1)}, f32[8,768]{1,0:T(8,128)S(1)}, u32[]{:S(2)}, u32[]{:S(2)}) collective-permute-start(f32[8,768]{1,0:T(8,128)S(1)} %get-tuple-element.111), channel_id=1, source_target_pairs={{0,28},{1,29},{2,30},{3,31},{4,32},{5,33},{6,34},{7,35},{8,36},{9,... | collective-permute-start | bytes 73736
  1088.4 40.0 %collective-permute-start.26 = (f32[8,768]{1,0:T(8,128)S(1)}, f32[8,768]{1,0:T(8,128)S(1)}, u32[]{:S(2)}, u32[]{:S(2)}) collective-permute-start(f32[8,768]{1,0:T(8,128)S(1)} %get-tuple-element.111), channel_id=1, source_target_pairs={{0,27},{1,28},{2,29},{3,30},{4,31},{5,32},{6,33},{7,34},{8,35},{9,... | collective-permute-start | bytes 73736
  1415.0 73.7 %collective-permute-start.96 = (f32[8,768]{1,0:T(8,128)}, f32[8,768]{1,0:T(8,128)S(1)}, u32[]{:S(2)}, u32[]{:S(2)}) collective-permute-start(f32[8,768]{1,0:T(8,128)} %get-tuple-element.114), channel_id=1, source_target_pairs={{0,1},{1,2},{2,3},{3,4},{4,5},{5,6},{6,7},{7,8},{8,9},{9,10},{10,1... | collective-permute-start | bytes 73736
  1417.6 84.5 %collective-permute-start.158 = (f32[8,3072]{1,0:T(8,128)S(1)}, f32[8,3072]{1,0:T(8,128)S(1)}, u32[]{:S(2)}, u32[]{:S(2)}) collective-permute-start(f32[8,3072]{1,0:T(8,128)S(1)} %get-tuple-element.115), channel_id=1, source_target_pairs={{0,31},{1,32},{2,33},{3,34},{4,35},{5,36},{6,37},{7,38},{8,39},{9,... | collective-permute-start | bytes 294920
  1418.9 86.3 %collective-permute-start.157 = (f32[8,3072]{1,0:T(8,128)S(1)}, f32[8,3072]{1,0:T(8,128)S(1)}, u32[]{:S(2)}, u32[]{:S(2)}) collective-permute-start(f32[8,3072]{1,0:T(8,128)S(1)} %get-tuple-element.115), channel_id=1, source_target_pairs={{0,30},{1,31},{2,32},{3,33},{4,34},{5,35},{6,36},{7,37},{8,38},{9,... | collective-permute-start | bytes 294920
  1420.2 73.2 %collective-permute-start.191 = (f32[6,3072]{1,0:T(8,128)S(1)}, f32[6,3072]{1,0:T(8,128)S(1)}, u32[]{:S(2)}, u32[]{:S(2)}) collective-permute-start(f32[6,3072]{1,0:T(8,128)S(1)} %slice.70), channel_id=1, source_target_pairs={{0,32},{1,33},{2,34},{3,35},{4,36},{5,37},{6,38},{7,39},{8,40},{9,... | collective-permute-start | bytes 221192
  1422.0 74.2 %collective-permute-start.159 = (f32[6,3072]{1,0:T(8,128)S(1)}, f32[6,3072]{1,0:T(8,128)S(1)}, u32[]{:S(2)}, u32[]{:S(2)}) collective-permute-start(f32[6,3072]{1,0:T(8,128)S(1)} %slice.69), channel_id=1, source_target_pairs={{0,32},{1,33},{2,34},{3,35},{4,36},{5,37},{6,38},{7,39},{8,40},{9,... | collective-permute-start | bytes 221192
  1540.2 39.8 %collective-permute-start.139 = (f32[8,3072]{1,0:T(8,128)S(1)}, f32[8,3072]{1,0:T(8,128)S(1)}, u32[]{:S(2)}, u32[]{:S(2)}) collective-permute-start(f32[8,3072]{1,0:T(8,128)S(1)} %get-tuple-element.115), channel_id=1, source_target_pairs={{0,12},{1,13},{2,14},{3,15},{4,16},{5,17},{6,18},{7,19},{8,20},{9,... | collective-permute-start | bytes 294920
  1542.2 40.1 %collective-permute-start.138 = (f32[8,3072]{1,0:T(8,128)S(1)}, f32[8,3072]{1,0:T(8,128)S(1)}, u32[]{:S(2)}, u32[]{:S(2)}) collective-permute-start(f32[8,3072]{1,0:T(8,128)S(1)} %get-tuple-element.115), channel_id=1, source_target_pairs={{0,11},{1,12},{2,13},{3,14},{4,15},{5,16},{6,17},{7,18},{8,19},{9,... | collective-permute-start | bytes 294920
  1546.4 40.2 %collective-permute-start.137 = (f32[8,3072]{1,0:T(8,128)S(1)}, f32[8,3072]{1,0:T(8,128)S(1)}, u32[]{:S(2)}, u32[]{:S(2)}) collective-permute-start(f32[8,3072]{1,0:T(8,128)S(1)} %get-tuple-element.115), channel_id=1, source_target_pairs={{0,10},{1,11},{2,12},{3,13},{4,14},{5,15},{6,16},{7,17},{8,18},{9,... | collective-permute-start | bytes 294920
  1582.3 39.5 %collective-permute-start.133 = (f32[8,3072]{1,0:T(8,128)S(1)}, f32[8,3072]{1,0:T(8,128)S(1)}, u32[]{:S(2)}, u32[]{:S(2)}) collective-permute-start(f32[8,3072]{1,0:T(8,128)S(1)} %get-tuple-element.115), channel_id=1, source_target_pairs={{0,6},{1,7},{2,8},{3,9},{4,10},{5,11},{6,12},{7,13},{8,14},{9,15},... | collective-permute-start | bytes 294920
  1611.6 42.7 %collective-permute-start.131 = (f32[8,3072]{1,0:T(8,128)S(1)}, f32[8,3072]{1,0:T(8,128)S(1)}, u32[]{:S(2)}, u32[]{:S(2)}) collective-permute-start(f32[8,3072]{1,0:T(8,128)S(1)} %get-tuple-element.115), channel_id=1, source_target_pairs={{0,4},{1,5},{2,6},{3,7},{4,8},{5,9},{6,10},{7,11},{8,12},{9,13},{1... | collective-permute-start | bytes 294920
  1613.5 43.2 %collective-permute-start.130 = (f32[8,3072]{1,0:T(8,128)S(1)}, f32[8,3072]{1,0:T(8,128)S(1)}, u32[]{:S(2)}, u32[]{:S(2)}) collective-permute-start(f32[8,3072]{1,0:T(8,128)S(1)} %get-tuple-element.115), channel_id=1, source_target_pairs={{0,3},{1,4},{2,5},{3,6},{4,7},{5,8},{6,9},{7,10},{8,11},{9,12},{10... | collective-permute-start | bytes 294920
  1619.1 39.5 %collective-permute-start.129 = (f32[8,3072]{1,0:T(8,128)S(1)}, f32[8,3072]{1,0:T(8,128)}, u32[]{:S(2)}, u32[]{:S(2)}) collective-permute-start(f32[8,3072]{1,0:T(8,128)S(1)} %get-tuple-element.115), channel_id=1, source_target_pairs={{0,2},{1,3},{2,4},{3,5},{4,6},{5,7},{6,8},{7,9},{8,10},{9,11},{10,... | collective-permute-start | bytes 294920
  1623.8 40.1 %collective-permute-start.190 = (f32[8,3072]{1,0:T(8,128)S(1)}, f32[8,3072]{1,0:T(8,128)}, u32[]{:S(2)}, u32[]{:S(2)}) collective-permute-start(f32[8,3072]{1,0:T(8,128)S(1)} %get-tuple-element.116), channel_id=1, source_target_pairs={{0,31},{1,32},{2,33},{3,34},{4,35},{5,36},{6,37},{7,38},{8,39},{9,... | collective-permute-start | bytes 294920
  1654.3 40.2 %collective-permute-start.189 = (f32[8,3072]{1,0:T(8,128)S(1)}, f32[8,3072]{1,0:T(8,128)}, u32[]{:S(2)}, u32[]{:S(2)}) collective-permute-start(f32[8,3072]{1,0:T(8,128)S(1)} %get-tuple-element.116), channel_id=1, source_target_pairs={{0,30},{1,31},{2,32},{3,33},{4,34},{5,35},{6,36},{7,37},{8,38},{9,... | collective-permute-start | bytes 294920
  1750.9 47.4 %collective-permute-start.164 = (f32[8,3072]{1,0:T(8,128)S(1)}, f32[8,3072]{1,0:T(8,128)}, u32[]{:S(2)}, u32[]{:S(2)}) collective-permute-start(f32[8,3072]{1,0:T(8,128)S(1)} %get-tuple-element.116), channel_id=1, source_target_pairs={{0,5},{1,6},{2,7},{3,8},{4,9},{5,10},{6,11},{7,12},{8,13},{9,14},{... | collective-permute-start | bytes 294920
  1752.8 45.5 %collective-permute-start.163 = (f32[8,3072]{1,0:T(8,128)S(1)}, f32[8,3072]{1,0:T(8,128)}, u32[]{:S(2)}, u32[]{:S(2)}) collective-permute-start(f32[8,3072]{1,0:T(8,128)S(1)} %get-tuple-element.116), channel_id=1, source_target_pairs={{0,4},{1,5},{2,6},{3,7},{4,8},{5,9},{6,10},{7,11},{8,12},{9,13},{1... | collective-permute-start | bytes 294920
  1754.8 43.5 %collective-permute-start.162 = (f32[8,3072]{1,0:T(8,128)S(1)}, f32[8,3072]{1,0:T(8,128)}, u32[]{:S(2)}, u32[]{:S(2)}) collective-permute-start(f32[8,3072]{1,0:T(8,128)S(1)} %get-tuple-element.116), channel_id=1, source_target_pairs={{0,3},{1,4},{2,5},{3,6},{4,7},{5,8},{6,9},{7,10},{8,11},{9,12},{10... | collective-permute-start | bytes 294920
  (373 other events, 25637.7 us)
Sparse Core Ops, SparseCore 0:
  11.4 67.8 all-gather.22
  82.7 61.5 all-gather.24
  147.7 61.5 all-gather.26
  212.6 61.6 all-gather.28
  276.3 21.9 all-gather.16
  300.4 25.4 all-gather.18
  329.4 69.0 all-gather.30
  402.1 65.8 all-gather.32
  471.4 64.6 all-gather.20
  565.3 29.7 reduce-scatter.20
  600.1 300.0 reduce-scatter.18
where the time goes:
time: 1900 us; the launch traced here: 1870 us
  blocking collectives  587 us (31%)
  starting transfers between devices  510 us (27%)
  waiting for transfers between devices  420 us (22%)
  local copies, waits for them, and re-layouts  232 us (12%)
  matrix products  67.1 us (4%)
  other arithmetic  35 us (2%)
  between operations  19.9 us (1%)
    unnamed x2, blocking collectives  526 us
    unnamed x193, starting transfers between devices  510 us
    unnamed x427, local copies, waits for them, and re-layouts  226 us
    all_gather x1, waiting for transfers between devices, shards(): lax.all_gather(w_gate.astype(bf), ('seq', 'dp'), axis=0, tiled=True)  65.2 us
    all_gather x1, waiting for transfers between devices, shards(): lax.all_gather(w_up.astype(bf), ('seq', 'dp'), axis=0, tiled=True)  61.7 us
    all_gather x1, waiting for transfers between devices, shards(): lax.all_gather(w_query.astype(bf), ('seq', 'dp'), axis=0, tiled=True)  61.2 us
    all_gather x1, waiting for transfers between devices, shards(): lax.all_gather(w_down.astype(bf), ('seq', 'dp'), axis=0, tiled=True)  54 us
    all_gather x1, waiting for transfers between devices, shards(): lax.all_gather(w_output.astype(bf), ('seq', 'dp'), axis=0, tiled=True)  53.8 us
  transfers between devices with their start and end apart: 203, of which 11 were waited for; matrix products, arithmetic and copies ran while one was open for 40% of the time, Pallas kernels for 0%

commit v1 on v0

v1 whole, which is shorter than its diff:
```python
import math

import jax
import jax.numpy as jnp
import numpy as np
from jax import lax
from jax.experimental import pallas as pl
from jax.experimental.pallas import tpu as pltpu
from jax.sharding import Mesh
from jax.sharding import PartitionSpec as P


BF = jnp.bfloat16
F32 = jnp.float32
HD = 64
D = 768
FF = 3072
HALF = 384
PACK = 1024
TOK = 256
LEN = 1024
HEADS = 6
EPS = 1e-05
MOMENTUM = 0.9
AVERAGE = 0.5
RATES = (0.01, 0.01, 0.01, 4.0, 0.02, 0.02, 0.015, 0.1)
MASKED = -1e30
AXES = ("z", "core", "y", "x")
VMEM_LIMIT = 60 * 1024 * 1024


def params():
    return pltpu.CompilerParams(vmem_limit_bytes=VMEM_LIMIT)


def device_pairs(move):
    pairs = []
    for z in range(4):
        for c in range(2):
            for y in range(4):
                for x in range(4):
                    to = move(z, c, y, x)
                    pairs.append((((z * 2 + c) * 4 + y) * 4 + x, ((to[0] * 2 + to[1]) * 4 + to[2]) * 4 + to[3]))
    return pairs


CORE_PAIRS = device_pairs(lambda z, c, y, x: (z, 1 - c, y, x))


def z_shift(k):
    return device_pairs(lambda z, c, y, x: ((z + k) % 4, c, y, x))


def halving_pairs(axis, first):
    def move(z, c, y, x):
        flip = 3 if (c == 0) == first else 1
        at = [z, c, y, x]
        at[axis] ^= flip
        return tuple(at)

    return device_pairs(move)


AXIS = {"z": 0, "y": 2, "x": 3}
ORDERS = (("x", "y", "z"), ("y", "z", "x"), ("z", "x", "y"))
LAST = ("x", "y", "z")


def permute(value, pairs):
    return lax.ppermute(value, AXES, pairs)


def chip_of_place(me, core):
    place = np.arange(64)
    rows = []
    for order in ORDERS:
        first = {axis: (place >> (5 - k)) & 1 for k, axis in enumerate(order)}
        second = {axis: (place >> (2 - k)) & 1 for k, axis in enumerate(LAST)}
        at = {}
        for axis in "zyx":
            one, two = jnp.asarray(first[axis]), jnp.asarray(second[axis])
            high = jnp.where(core == 0, one, two)
            low = jnp.where(core == 0, two, one)
            mine = me[axis]
            high = high ^ (mine >> 1)
            low = low ^ ((mine >> 1) ^ (mine & 1))
            at[axis] = high * 2 + (high ^ low)
        rows.append(at["z"] * 16 + at["y"] * 4 + at["x"])
    return jnp.stack(rows).astype(jnp.int32)


def spread_matrix():
    feature = lax.broadcasted_iota(jnp.int32, (HALF, 512), 0)
    place = lax.broadcasted_iota(jnp.int32, (HALF, 512), 1)
    z, rest = place // 256, place % 256
    yx, core, row = rest // 16, (rest // 8) % 2, rest % 8
    want = ((z * 2 + core) * 16 + yx) * 6 + row
    return ((feature == want) & (row < 6)).astype(BF)


def dot(left, right):
    return jnp.dot(left, right, preferred_element_type=F32)


def dot_nt(left, right):
    return lax.dot_general(left, right, (((1,), (1,)), ((), ())), preferred_element_type=F32)


def dot_tn(left, right):
    return lax.dot_general(left, right, (((0,), (0,)), ((), ())), preferred_element_type=F32)


def spread(values, e2):
    return jnp.concatenate([dot(values[:, :HALF], e2), dot(values[:, HALF:], e2)], axis=1).astype(BF)


def gather_back(values, e2):
    high = values.astype(BF)
    low = (values - high.astype(F32)).astype(BF)
    return jnp.concatenate(
        [dot_nt(high[:, k : k + 512], e2) + dot_nt(low[:, k : k + 512], e2) for k in (0, 512)], axis=1
    )


def swap_halves(tile):
    lane = lax.broadcasted_iota(jnp.int32, tile.shape, 1)
    return jnp.where(lane % HD < HD // 2, pltpu.roll(tile, 96, 1), pltpu.roll(tile, 32, 1))


def lanes_of(tile, odd):
    lane = lax.broadcasted_iota(jnp.int32, tile.shape, 1)
    return jnp.where((lane >= HD) == bool(odd), tile, jnp.zeros_like(tile))


def join_lanes(even, odd):
    lane = lax.broadcasted_iota(jnp.int32, even.shape, 1)
    return jnp.where(lane < HD, even, odd)


def pack_kernel(scal, wq, wk, wv, wo, wg, wu, wd, gains, keep, send, down):
    core = scal[1]
    k = 0
    for w in (wq, wk, wv, wo, wg, wu):
        count = w.shape[1] // D
        for part in range(count):
            halves = [w[:, part * D + h * HALF : part * D + (h + 1) * HALF] for h in range(2)]
            keep[k, 0:6, :] = jnp.where(core == 0, halves[0], halves[1])
            send[k, 0:6, :] = jnp.where(core == 0, halves[1], halves[0])
            keep[k, 6:8, :] = jnp.zeros((2, HALF), F32)
            send[k, 6:8, :] = jnp.zeros((2, HALF), F32)
            k += 1
    lane = lax.broadcasted_iota(jnp.int32, (6, HALF), 1)
    row = lax.broadcasted_iota(jnp.int32, (6, HALF), 0)
    here = lane == row + core * 8
    for col in range(2):
        line = jnp.sum(jnp.where(here, gains[:, col : col + 1], 0.0), axis=0, keepdims=True)
        keep[0, 6 + col : 7 + col, :] = line
        send[0, 6 + col : 7 + col, :] = line
    for j in range(3):
        rows = wd[8 * j : 8 * j + 8, :]
        down[j] = jnp.concatenate([rows[:, :HALF], rows[:, HALF:]], axis=0).astype(BF)


def attn_forward_kernel(
    scal, xp, gq, gk, gv, cosine, sine, start, e2, q_all, k_all, v_all, h1_own, probs, o_out, g1_out, g2_out, h1p, bias
):
    z = scal[0]
    own = pl.multiple_of(z * TOK, TOK)
    held = gq[:, 0, :, 0:128].astype(F32)
    rows = lax.broadcasted_iota(jnp.int32, held.shape, 1)
    lane = lax.broadcasted_iota(jnp.int32, held.shape, 2)
    chip = lax.broadcasted_iota(jnp.int32, (64, PACK), 0)
    place = lax.broadcasted_iota(jnp.int32, (64, PACK), 1)
    take = lax.broadcasted_iota(jnp.int32, (128, PACK), 0)
    fold = (take == lax.broadcasted_iota(jnp.int32, (128, PACK), 1) % 16).astype(BF)
    lines = []
    for k in range(2):
        wanted = (rows == jnp.where(lane < 8, 6 + k, 14 + k)) & (lane < 16)
        table = jnp.sum(jnp.where(wanted, held, 0.0), axis=1).astype(BF)
        wide = dot(table, fold)
        lines.append(jnp.sum(jnp.where(place // 16 == chip, wide, 0.0), axis=0, keepdims=True))
    g1 = lines[0]
    g1_out[...] = jnp.broadcast_to(g1, (8, PACK))
    g2 = jnp.broadcast_to(lines[1], (8, PACK)).astype(BF)
    g2_out[...] = jnp.concatenate([dot_nt(g2[:, :512], e2[...]), dot_nt(g2[:, 512:], e2[...])], axis=1)

    wq, wk, wv = (w[...].reshape(PACK, HALF) for w in (gq, gk, gv))

    def block(b, carry):
        at = pl.ds(pl.multiple_of(b * TOK, TOK), TOK)
        x = xp[at, :].astype(F32)
        scale = lax.rsqrt(jnp.sum(x * x, axis=1, keepdims=True) * (1.0 / D) + EPS)
        h1 = (x * scale * g1).astype(BF)
        h1p[at, :] = h1
        cs, sn = cosine[at, :], sine[at, :]
        for w, out, factor in ((wq, q_all, 0.125), (wk, k_all, 1.0)):
            raw = dot(h1, w)
            for t in range(3):
                u = raw[:, 128 * t : 128 * t + 128]
                turned = (u * cs + swap_halves(u) * sn).astype(BF)
                out[at, 128 * t : 128 * t + 128] = turned * BF(factor)
        v_all[at, :] = dot(h1, wv).astype(BF)
        return carry

    lax.fori_loop(0, 4, block, 0)
    h1_own[...] = h1p[pl.ds(own, TOK), :]

    key = lax.broadcasted_iota(jnp.int32, (TOK, LEN), 1).astype(F32)
    query = (lax.broadcasted_iota(jnp.int32, (TOK, LEN), 0) + own).astype(F32)
    first = start[pl.ds(own, TOK), :]
    bias[...] = jnp.where((key >= first) & (key <= query), 0.0, MASKED)
    lane = lax.broadcasted_iota(jnp.int32, (TOK, 128), 1)
    logs = jnp.zeros((TOK, 128), F32)
    for t in range(3):
        cols = slice(128 * t, 128 * t + 128)
        q_tile = q_all[pl.ds(own, TOK), cols]
        k_tile = k_all[:, cols]
        v_tile = v_all[:, cols]
        mixed = []
        for odd in range(2):
            h = 2 * t + odd
            s = dot_nt(lanes_of(q_tile, odd), k_tile) + bias[...]
            top = jnp.max(s, axis=1, keepdims=True)
            expo = jnp.exp(s - top)
            total = jnp.sum(expo, axis=1, keepdims=True)
            pb = (expo * (1.0 / total)).astype(BF)
            probs[h] = pb
            mixed.append(dot(pb, v_tile))
            logs = jnp.where(lane == h, top + jnp.log(total), logs)
        o_out[:, cols] = join_lanes(mixed[0], mixed[1]).astype(BF)
    high = logs.astype(BF).astype(F32)
    mid = (logs - high).astype(BF).astype(F32)
    low = logs - high - mid
    packed = jnp.where(lane < 8, high, jnp.where(lane < 16, pltpu.roll(mid, 8, 1), pltpu.roll(low, 16, 1)))
    o_out[:, HALF:] = jnp.where(lane < 24, packed, 0.0).astype(BF)


def attn_out_kernel(scal, o, wo_keep, wo_other, e2, part):
    core = scal[1]
    spread_o = dot(o[:, :HALF], e2[...]).astype(BF)
    mine = dot(spread_o, wo_keep[...].reshape(512, HALF))
    other = dot(spread_o, wo_other[...].reshape(512, HALF))
    part[:, :HALF] = jnp.where(core == 0, mine, other)
    part[:, HALF:] = jnp.where(core == 0, other, mine)


def ffn_kernel(
    scal,
    chips,
    x,
    part_a,
    part_b,
    dy,
    e2,
    g2,
    wg,
    wu,
    wd,
    out_keep,
    out_send,
    dh2_out,
    resid,
    gg2,
    keep_g,
    send_g,
    keep_u,
    send_u,
    keep_d,
    send_d,
    h2p,
    h2p_t,
    acc_out,
    acc_dh2,
    grad,
    grad_d,
):
    core = scal[1]
    j = pl.program_id(0)

    @pl.when(j == 0)
    def _():
        r = x[...].astype(F32) + (part_a[...] + part_b[...])
        resid[...] = r
        scale = lax.rsqrt(jnp.mean(r * r, axis=1, keepdims=True) + EPS)
        h2 = (r * scale * g2[0:1, :]).astype(BF)
        packed = spread(h2, e2[...])
        h2p[...] = packed
        h2p_t[...] = packed.T
        acc_out[...] = jnp.zeros_like(acc_out)
        acc_dh2[...] = jnp.zeros_like(acc_dh2)

    w_gate = wg[...].reshape(PACK, HALF)
    w_up = wu[...].reshape(PACK, HALF)
    blocks = wd[...].astype(F32)
    w_down = jnp.concatenate(
        [blocks[:, :, 0:8, :].reshape(HALF, HALF), blocks[:, :, 8:16, :].reshape(HALF, HALF)], axis=1
    ).astype(BF)
    h2 = h2p[...]
    gate = dot(h2, w_gate)
    up = dot(h2, w_up)
    sig = jax.nn.sigmoid(gate)
    hidden = (gate * sig * up).astype(BF)
    acc_out[...] += dot(hidden, w_down)
    dhid = dot_nt(dy[...], w_down)
    dgate = (dhid * up * sig * (1.0 + gate * (1.0 - sig))).astype(BF)
    dup = (dhid * gate * sig).astype(BF)
    acc_dh2[...] += dot_nt(dgate, w_gate) + dot_nt(dup, w_up)

    for part, value, keep, send in ((0, dgate, keep_g, send_g), (1, dup, keep_u, send_u)):
        grad[...] = dot(h2p_t[...], value)

        def write(w, carry, part=part, keep=keep, send=send):
            a = pl.multiple_of(chips[part, w] * 16, 16)
            b = pl.multiple_of(chips[part, w + 32] * 16, 16)
            keep[w, 0] = grad[pl.ds(a, 16), :].astype(BF)
            send[w, 0] = grad[pl.ds(b, 16), :].astype(BF)
            return carry

        lax.fori_loop(0, 32, write, 0)
    grad_d[pl.ds(pl.multiple_of(j * HALF, HALF), HALF), :] = dot_tn(hidden, dy[...])

    @pl.when(j == 3)
    def _():
        mine = pl.multiple_of(core * 128, 128)
        other = pl.multiple_of((1 - core) * 128, 128)
        out_keep[...] = acc_out[pl.ds(mine, 128), :]
        out_send[...] = acc_out[pl.ds(other, 128), :]
        dh2 = gather_back(acc_dh2[...], e2[...])
        dh2_out[...] = dh2
        r = resid[...]
        scale = lax.rsqrt(jnp.mean(r * r, axis=1, keepdims=True) + EPS)
        gg2[...] = jnp.broadcast_to(jnp.sum(dh2 * r * scale, axis=0, keepdims=True), (8, D))

        def write(w, carry):
            for at, out in ((w, keep_d), (w + 32, send_d)):
                base = chips[2, at] * 24
                for k in range(3):
                    rows = grad_d[pl.ds(pl.multiple_of(base + 8 * k, 8), 8), :]
                    out[w, k] = jnp.concatenate([rows[:, :HALF], rows[:, HALF:]], axis=0).astype(BF)
            return carry

        lax.fori_loop(0, 32, write, 0)


def resid_backward_kernel(scal, resid, dh2_a, dh2_b, g2, dy, wo_keep, wo_other, e2, dres_out, dresb_out, do_out):
    core = scal[1]
    r = resid[...]
    dh2 = dh2_a[...] + dh2_b[...]
    scale = lax.rsqrt(jnp.mean(r * r, axis=1, keepdims=True) + EPS)
    weighted = dh2 * g2[0:1, :]
    inner = jnp.mean(weighted * r, axis=1, keepdims=True)
    dres = dy[...].astype(F32) + (scale * weighted - r * (scale * scale * scale) * inner)
    mine = pl.multiple_of(core * 128, 128)
    dresb = dres.astype(BF)
    dresb_out[...] = dresb
    d_mine = jnp.where(core == 0, dresb[:, :HALF], dresb[:, HALF:])
    d_other = jnp.where(core == 0, dresb[:, HALF:], dresb[:, :HALF])
    do = dot_nt(d_mine, wo_keep[...].reshape(512, HALF)) + dot_nt(d_other, wo_other[...].reshape(512, HALF))
    do_out[...] = dot_nt(do.astype(BF), e2[...]).astype(BF)
    resid_rows = dres
    dres_out[0] = resid_rows[0:128, :]
    dres_out[1] = resid_rows[128:256, :]
    del mine


def attn_query_kernel(scal, probs, do, o, k_all, v_all, cosine, sine, dq_out):
    own = pl.multiple_of(scal[0] * TOK, TOK)
    cs, sn = cosine[pl.ds(own, TOK), :], sine[pl.ds(own, TOK), :]
    for t in range(3):
        cols = slice(128 * t, 128 * t + 128)
        do_tile = do[:, cols]
        product = do_tile.astype(F32) * o[:, cols].astype(F32)
        k_tile, v_tile = k_all[:, cols], v_all[:, cols]
        both = []
        for odd in range(2):
            inner = jnp.sum(lanes_of(product, odd), axis=1, keepdims=True)
            dp = dot_nt(lanes_of(do_tile, odd), v_tile)
            ds = (probs[2 * t + odd].astype(F32) * (dp - inner)).astype(BF)
            both.append(dot(ds, k_tile))
        u = join_lanes(both[0], both[1]) * 0.125
        dq_out[:, cols] = (u * cs - swap_halves(u) * sn).astype(BF)


def attn_key_kernel(
    scal, q_all, k_all, v_all, do0, do1, do2, do3, o0, o1, o2, o3, start, cosine, sine, dk_out, dv_out, dk_acc, dv_acc
):
    z = scal[0]
    own = pl.multiple_of(z * TOK, TOK)
    head = lax.broadcasted_iota(jnp.int32, (8, 128), 0)
    lane = lax.broadcasted_iota(jnp.int32, (8, 128), 1)
    pick = ((lane < 24) & (lane % 8 == head)).astype(BF)
    head_of = (
        lax.broadcasted_iota(jnp.int32, (8, HALF), 1) // HD == lax.broadcasted_iota(jnp.int32, (8, HALF), 0)
    ).astype(F32)
    dk_acc[...] = jnp.zeros_like(dk_acc)
    dv_acc[...] = jnp.zeros_like(dv_acc)
    key = (lax.broadcasted_iota(jnp.int32, (TOK, TOK), 0) + own).astype(F32)
    for k, (do, o) in enumerate(((do0, o0), (do1, o1), (do2, o2), (do3, o3))):
        zq = lax.rem(z + 4 - k, 4)

        @pl.when(zq >= z)
        def _(do=do, o=o, zq=zq):
            at = pl.multiple_of(zq * TOK, TOK)
            logs = dot_nt(pick, o[:, HALF:])
            inner = lax.dot_general(
                head_of,
                do[...].astype(F32) * o[:, :HALF].astype(F32),
                (((1,), (1,)), ((), ())),
                precision=lax.Precision.HIGHEST,
                preferred_element_type=F32,
            )
            query = (lax.broadcasted_iota(jnp.int32, (TOK, TOK), 1) + at).astype(F32)
            seen = (key >= start[0:1, pl.ds(at, TOK)]) & (key <= query)
            bias = jnp.where(seen, 0.0, MASKED)
            for t in range(3):
                cols = slice(128 * t, 128 * t + 128)
                q_tile, do_tile = q_all[pl.ds(at, TOK), cols], do[:, cols]
                k_tile, v_tile = k_all[pl.ds(own, TOK), cols], v_all[pl.ds(own, TOK), cols]
                dks, dvs = [], []
                for odd in range(2):
                    h = 2 * t + odd
                    s = dot_nt(lanes_of(k_tile, odd), q_tile) + bias
                    p = jnp.exp(s - logs[h : h + 1, :])
                    dvs.append(dot(p.astype(BF), do_tile))
                    dp = dot_nt(lanes_of(v_tile, odd), do_tile)
                    ds = (p * (dp - inner[h : h + 1, :])).astype(BF)
                    dks.append(dot(ds, q_tile))
                dk_acc[:, cols] += join_lanes(dks[0], dks[1])
                dv_acc[:, cols] += join_lanes(dvs[0], dvs[1])

    cs, sn = cosine[pl.ds(own, TOK), :], sine[pl.ds(own, TOK), :]
    for t in range(3):
        cols = slice(128 * t, 128 * t + 128)
        u = dk_acc[:, cols]
        dk_out[:, cols] = (u * cs - swap_halves(u) * sn).astype(BF)
    dv_out[...] = dv_acc[...].astype(BF)


def attn_grads_kernel(
    scal,
    chips,
    dq,
    dk,
    dv,
    xp,
    h1,
    o_mine,
    o_other,
    dresb,
    gg2,
    gq,
    gk,
    gv,
    e2,
    dh1_keep,
    dh1_send,
    k0,
    k1,
    k2,
    s0,
    s1,
    s2,
    grad,
    grad_o,
    lines,
    dh1,
):
    core = scal[1]
    own = pl.multiple_of(scal[0] * TOK, TOK)
    e = e2[...]
    wq, wk, wv = (w[...].reshape(PACK, HALF) for w in (gq, gk, gv))
    dh1[...] = dot_nt(dq[...], wq) + dot_nt(dk[...], wk) + dot_nt(dv[...], wv)
    dh1_keep[...] = dh1[pl.ds(pl.multiple_of(core * 128, 128), 128), :]
    dh1_send[...] = dh1[pl.ds(pl.multiple_of((1 - core) * 128, 128), 128), :]
    x = xp[pl.ds(own, TOK), :].astype(F32)
    scale = lax.rsqrt(jnp.sum(x * x, axis=1, keepdims=True) * (1.0 / D) + EPS)
    gg1 = jnp.sum(dh1[...] * x * scale, axis=0, keepdims=True)
    g2_wide = spread(gg2[...].astype(BF), e).astype(F32)[0:1, :]
    chip = lax.broadcasted_iota(jnp.int32, (64, PACK), 0)
    place = lax.broadcasted_iota(jnp.int32, (64, PACK), 1)
    fold = (
        lax.broadcasted_iota(jnp.int32, (128, PACK), 0) == lax.broadcasted_iota(jnp.int32, (128, PACK), 1) % 16
    ).astype(BF)
    for k, line in enumerate((gg1, g2_wide)):
        lines[k] = dot_nt(jnp.where(place // 16 == chip, line, 0.0).astype(BF), fold)

    h1_t = h1[...].T
    for p, value in enumerate((dq, dk, dv)):
        grad[p] = dot(h1_t, value[...])
    o_a, o_b = o_mine[:, :HALF], o_other[:, :HALF]
    o_full = jnp.concatenate(
        [dot(jnp.where(core == 0, o_a, o_b), e), dot(jnp.where(core == 0, o_b, o_a), e)], axis=1
    ).astype(BF)
    d_mine = jnp.where(core == 0, dresb[:, :HALF], dresb[:, HALF:])
    grad_o[...] = dot_tn(o_full, d_mine)

    row = lax.broadcasted_iota(jnp.int32, (16, 128), 0)
    lane = lax.broadcasted_iota(jnp.int32, (16, 128), 1)
    row_one = row == jnp.where(lane < 8, 6, 14)
    row_two = row == jnp.where(lane < 8, 7, 15)
    used = lane < 16

    def write(w, carry):
        for p, (keep, send) in enumerate(((k0, s0), (k1, s1), (k2, s2))):
            for at, out in ((w, keep), (w + 32, send)):
                i = chips[p, at]
                base = pl.multiple_of(i * 16, 16)
                block = grad[p, pl.ds(base, 16), :]
                if p == 0:
                    tile = block[:, :128]
                    tile = jnp.where(used & row_one, lines[0, pl.ds(i, 1), :], tile)
                    tile = jnp.where(used & row_two, lines[1, pl.ds(i, 1), :], tile)
                    out[w, :, 0:128] = tile.astype(BF)
                    out[w, :, 128:HALF] = block[:, 128:].astype(BF)
                else:
                    out[w, :, 0:HALF] = block.astype(BF)
                out[w, :, HALF:512] = grad_o[pl.ds(base, 16), 128 * p : 128 * p + 128].astype(BF)
        return carry

    lax.fori_loop(0, 32, write, 0)


def token_outputs_kernel(scal, xp, dh1_a, dh1_b, g1, dres, e2, resid, out_a, out_b, output, input_grad):
    core = scal[1]
    at = pl.multiple_of(scal[0] * TOK + core * 128, 128)
    x = xp[pl.ds(at, 128), :].astype(F32)
    scale = lax.rsqrt(jnp.sum(x * x, axis=1, keepdims=True) * (1.0 / D) + EPS)
    weighted = (dh1_a[...] + dh1_b[...]) * g1[0:1, :]
    inner = jnp.sum(weighted * x, axis=1, keepdims=True) * (1.0 / D)
    dx = scale * weighted - x * (scale * scale * scale) * inner
    input_grad[...] = dres[core] + gather_back(dx, e2[...])
    mine = pl.ds(pl.multiple_of(core * 128, 128), 128)
    output[...] = (resid[mine, :] + (out_a[...] + out_b[...])).astype(BF)


def update_kernel(scal, attn_a, attn_b, ff_a, ff_b, *refs):
    core = scal[1]
    masters, moments, averages = refs[0:8], refs[8:16], refs[16:24]
    news, moms, means, copies = refs[24:32], refs[32:40], refs[40:48], refs[48:56]
    base = 1.0 / math.sqrt(16384)

    def step(k, at, grad):
        rate = RATES[k] * base
        moment = MOMENTUM * moments[k][at] + grad
        new = masters[k][at] - rate * (grad + MOMENTUM * moment)
        news[k][at] = new
        moms[k][at] = moment
        means[k][at] = AVERAGE * averages[k][at] + (1.0 - AVERAGE) * new
        copies[k][at] = new.astype(BF)

    def halves(a, b):
        return (jnp.where(core == 0, a, b), jnp.where(core == 0, b, a))

    for p in range(3):
        lo = 512 * p
        for h, grad in enumerate(halves(attn_a[0:6, lo : lo + HALF], attn_b[0:6, lo : lo + HALF])):
            step(p, (slice(0, 6), slice(h * HALF, (h + 1) * HALF)), grad)
        lo = 512 * p + HALF
        for h, grad in enumerate(halves(attn_a[0:6, lo : lo + 128], attn_b[0:6, lo : lo + 128])):
            at = h * HALF + 128 * p
            step(3, (slice(0, 6), slice(at, at + 128)), grad)
    for k in range(2):
        for j in range(4):
            for h, grad in enumerate(halves(ff_a[4 * k + j, 0:6, :], ff_b[4 * k + j, 0:6, :])):
                at = j * D + h * HALF
                step(4 + k, (slice(0, 6), slice(at, at + HALF)), grad)
    for j in range(3):
        for h in range(2):
            grad = ff_a[8 + j, 8 * h : 8 * h + 8, :]
            step(6, (slice(8 * j, 8 * j + 8), slice(h * HALF, (h + 1) * HALF)), grad)
    both = attn_a[6:8, 0:128] + attn_b[6:8, 0:128]
    row = lax.broadcasted_iota(jnp.int32, (6, 128), 0)
    lane = lax.broadcasted_iota(jnp.int32, (6, 128), 1)
    here = lane == row + 8 * core
    for col in range(2):
        grad = jnp.sum(jnp.where(here, both[col : col + 1, :], 0.0), axis=1, keepdims=True)
        step(7, (slice(0, 6), slice(col, col + 1)), grad)


def whole():
    return pl.BlockSpec(memory_space=pltpu.VMEM)


def scalars():
    return pl.BlockSpec(memory_space=pltpu.SMEM)


def call(kernel, out_shape, operands, scratch=(), smem=1, name=None):
    specs = [scalars() if k < smem else whole() for k in range(len(operands))]
    return pl.pallas_call(
        kernel,
        out_shape=out_shape,
        in_specs=specs,
        out_specs=jax.tree.map(lambda _: whole(), out_shape),
        scratch_shapes=list(scratch),
        compiler_params=params(),
        name=name,
    )(*operands)


def shape(dims, kind):
    return jax.ShapeDtypeStruct(dims, kind)


def halving(keep, send, steps):
    for k, (axis, first) in enumerate(steps):
        got = permute(send, halving_pairs(AXIS[axis], first))
        count = keep.shape[0] // 2
        total = keep.astype(F32) + got.astype(F32)
        if count == 0 or k == len(steps) - 1:
            return total
        total = total.astype(BF)
        keep, send = total[:count], total[count:]
    return keep


def reduce_parts(parts, join_axis):
    thirds = []
    for order, (keep, send) in zip(ORDERS, parts):
        thirds.append(halving(keep, send, [(axis, True) for axis in order]))
    joined = jnp.concatenate([t.astype(BF) for t in thirds], axis=join_axis)
    return halving(joined[:4], joined[4:], [(axis, False) for axis in LAST])[0]


def shards(inputs, doc_ids, cotangent, *state):
    masters, moments, averages = state[0:8], state[8:16], state[16:24]
    z, core = lax.axis_index("z"), lax.axis_index("core")
    y, x_at = lax.axis_index("y"), lax.axis_index("x")
    scal = jnp.stack([z, core]).astype(jnp.int32)
    chips = chip_of_place({"z": z, "y": y, "x": x_at}, core)
    e2 = spread_matrix()

    def by_core(mine, other, axis):
        return jnp.where(
            core == 0, jnp.concatenate([mine, other], axis=axis), jnp.concatenate([other, mine], axis=axis)
        )

    keep, send, down = call(
        pack_kernel,
        (shape((12, 8, HALF), F32), shape((12, 8, HALF), F32), shape((3, 16, HALF), BF)),
        (scal, *masters),
        name="pack_weights",
    )
    packed = by_core(keep, permute(send, CORE_PAIRS), 1).astype(BF)
    packed = jnp.concatenate([packed, down], axis=0)
    gathered = lax.all_gather(packed, ("z", "y", "x"), axis=0, tiled=False)

    ids_row = jnp.zeros((16, D), BF).at[0, :128].set(doc_ids[0].astype(BF))
    block = jnp.concatenate([inputs[0], ids_row], axis=0)
    ring = [block] + [permute(block, z_shift(k)) for k in (1, 2, 3)]
    ring = jnp.stack(ring)
    both = by_core(ring[:, None], permute(ring, CORE_PAIRS)[:, None], 1)
    both = jnp.roll(both[::-1], z + 1, axis=0)
    x_all = both[:, :, :128].reshape(LEN, D)
    ids = both[:, :, 128, :128].reshape(LEN).astype(F32)
    dy = by_core(cotangent[0], permute(cotangent[0], CORE_PAIRS), 0)
    starts = jnp.sum((ids[None, :] < ids[:, None]).astype(jnp.int32), axis=1)
    places = (jnp.arange(LEN, dtype=jnp.int32) - starts).astype(F32)
    freq = 10000.0 ** (-jnp.arange(0, HD, 2, dtype=F32) / HD)
    theta = places[:, None] * freq[None, :]
    cosine, sine = jnp.cos(theta), jnp.sin(theta)
    cosine = jnp.concatenate([cosine] * 4, axis=1)
    sine = jnp.concatenate([-sine, sine, -sine, sine], axis=1)
    start_col = starts.astype(F32)[:, None]
    start_row = jnp.broadcast_to(starts.astype(F32)[None, :], (8, LEN))
    xp = jnp.concatenate(
        [jnp.dot(x_all[:, :HALF], e2, preferred_element_type=F32), jnp.dot(x_all[:, HALF:], e2, preferred_element_type=F32)],
        axis=1,
    ).astype(BF)
    x_chip = lax.dynamic_slice_in_dim(x_all, z * TOK, TOK, 0)

    def chunk(k):
        return pl.BlockSpec((64, 1, 16, HALF), lambda i, k=k: (0, k, 0, 0))

    def full(dims):
        return pl.BlockSpec(dims, lambda i, n=len(dims): (0,) * n)

    forward_out = (
        shape((LEN, HALF), BF),
        shape((LEN, HALF), BF),
        shape((LEN, HALF), BF),
        shape((TOK, PACK), BF),
        shape((HEADS, TOK, LEN), BF),
        shape((TOK, 512), BF),
        shape((8, PACK), F32),
        shape((8, D), F32),
    )
    q_all, k_all, v_all, h1_own, probs, o, g1, g2 = pl.pallas_call(
        attn_forward_kernel,
        out_shape=forward_out,
        grid=(1,),
        in_specs=[
            scalars(),
            full((LEN, PACK)),
            chunk(0),
            chunk(1),
            chunk(2),
            full((LEN, 128)),
            full((LEN, 128)),
            full((LEN, 1)),
            full((HALF, 512)),
        ],
        out_specs=tuple(full(s.shape) for s in forward_out),
        scratch_shapes=[pltpu.VMEM((LEN, PACK), BF), pltpu.VMEM((TOK, LEN), F32)],
        compiler_params=params(),
        name="attention_forward",
    )(scal, xp, gathered, gathered, gathered, cosine, sine, start_col, e2)

    wo_keep = lax.dynamic_slice_in_dim(gathered, core * 32, 32, 0)[:, 3]
    wo_send = lax.dynamic_slice_in_dim(gathered, (1 - core) * 32, 32, 0)[:, 3]
    wo_other = permute(wo_send, CORE_PAIRS)
    part = call(attn_out_kernel, shape((TOK, D), F32), (scal, o, wo_keep, wo_other, e2), name="attention_output")
    part_other = permute(part, CORE_PAIRS)

    ffn_out = (
        shape((128, D), F32),
        shape((128, D), F32),
        shape((TOK, D), F32),
        shape((TOK, D), F32),
        shape((8, D), F32),
    ) + tuple(shape((32, 4, 16, HALF), BF) for _ in range(4)) + tuple(shape((32, 3, 16, HALF), BF) for _ in range(2))
    column = pl.BlockSpec((32, 1, 16, HALF), lambda j: (0, j, 0, 0))
    out_keep, out_send, dh2, resid, gg2, kg, sg, ku, su, kd, sd = pl.pallas_call(
        ffn_kernel,
        out_shape=ffn_out,
        grid=(4,),
        in_specs=[
            scalars(),
            scalars(),
            full((TOK, D)),
            full((TOK, D)),
            full((TOK, D)),
            full((TOK, D)),
            full((HALF, 512)),
            full((8, D)),
            pl.BlockSpec((64, 1, 16, HALF), lambda j: (0, 4 + j, 0, 0)),
            pl.BlockSpec((64, 1, 16, HALF), lambda j: (0, 8 + j, 0, 0)),
            pl.BlockSpec((16, 3, 16, HALF), lambda j: (j, 4, 0, 0)),
        ],
        out_specs=tuple(full(s.shape) for s in ffn_out[:5])
        + (column,) * 4
        + tuple(full(s.shape) for s in ffn_out[9:]),
        scratch_shapes=[
            pltpu.VMEM((TOK, PACK), BF),
            pltpu.VMEM((PACK, TOK), BF),
            pltpu.VMEM((TOK, D), F32),
            pltpu.VMEM((TOK, PACK), F32),
            pltpu.VMEM((PACK, HALF), F32),
            pltpu.VMEM((FF // 2, D), F32),
        ],
        compiler_params=params(),
        name="feed_forward",
    )(scal, chips, x_chip, part, part_other, dy, e2, g2, gathered, gathered, gathered)

    dh2_other = permute(dh2, CORE_PAIRS)
    out_other = permute(out_send, CORE_PAIRS)
    o_other = permute(o, CORE_PAIRS)
    o_ring = [o] + [permute(o, z_shift(k)) for k in (1, 2, 3)]
    ff_block = reduce_parts(((kg, sg), (ku, su), (kd, sd)), 1)

    dres, dresb, do = call(
        resid_backward_kernel,
        (shape((2, 128, D), F32), shape((TOK, D), BF), shape((TOK, HALF), BF)),
        (scal, resid, dh2, dh2_other, g2, dy, wo_keep, wo_other, e2),
        name="residual_backward",
    )
    do_ring = [do] + [permute(do, z_shift(k)) for k in (1, 2, 3)]
    dq = call(
        attn_query_kernel,
        shape((TOK, HALF), BF),
        (scal, probs, do, o, k_all, v_all, cosine, sine),
        name="attention_query_gradient",
    )
    dk, dv = call(
        attn_key_kernel,
        (shape((TOK, HALF), BF), shape((TOK, HALF), BF)),
        (scal, q_all, k_all, v_all, *do_ring, *o_ring, start_row, cosine, sine),
        scratch=(pltpu.VMEM((TOK, HALF), F32), pltpu.VMEM((TOK, HALF), F32)),
        name="attention_key_gradient",
    )
    grads_out = (shape((128, PACK), F32),) * 2 + (shape((32, 16, 512), BF),) * 6
    dh1, dh1_send, k0, k1, k2, s0, s1, s2 = pl.pallas_call(
        attn_grads_kernel,
        out_shape=grads_out,
        grid=(1,),
        in_specs=[
            scalars(),
            scalars(),
            full((TOK, HALF)),
            full((TOK, HALF)),
            full((TOK, HALF)),
            full((LEN, PACK)),
            full((TOK, PACK)),
            full((TOK, 512)),
            full((TOK, 512)),
            full((TOK, D)),
            full((8, D)),
            chunk(0),
            chunk(1),
            chunk(2),
            full((HALF, 512)),
        ],
        out_specs=tuple(full(s.shape) for s in grads_out),
        scratch_shapes=[
            pltpu.VMEM((3, PACK, HALF), F32),
            pltpu.VMEM((PACK, HALF), F32),
            pltpu.VMEM((2, 64, 128), F32),
            pltpu.VMEM((TOK, PACK), F32),
        ],
        compiler_params=params(),
        name="attention_weight_gradients",
    )(scal, chips, dq, dk, dv, xp, h1_own, o, o_other, dresb, gg2, gathered, gathered, gathered, e2)
    dh1_other = permute(dh1_send, CORE_PAIRS)
    attn_block = reduce_parts(((k0, s0), (k1, s1), (k2, s2)), 2)

    output, input_grad = call(
        token_outputs_kernel,
        (shape((128, D), BF), shape((128, D), F32)),
        (scal, xp, dh1, dh1_other, g1, dres, e2, resid, out_keep, out_other),
        name="token_outputs",
    )

    attn_rows = attn_block.reshape(2, 8, 3 * 512)
    ff_rows = ff_block[:8].reshape(8, 2, 8, HALF)
    attn_mine = lax.dynamic_index_in_dim(attn_rows, core, 0, False)
    attn_theirs = permute(lax.dynamic_index_in_dim(attn_rows, 1 - core, 0, False), CORE_PAIRS)
    ff_mine = lax.dynamic_index_in_dim(ff_rows, core, 1, False)
    ff_theirs = permute(lax.dynamic_index_in_dim(ff_rows, 1 - core, 1, False), CORE_PAIRS)
    pad = jnp.zeros((8, 8, HALF), F32)
    ff_mine = jnp.concatenate([jnp.concatenate([ff_mine, pad], axis=1), ff_block[8:]], axis=0)
    shapes = tuple(shape(m.shape, F32) for m in masters)
    outs = call(
        update_kernel,
        shapes * 3 + tuple(shape(m.shape, BF) for m in masters),
        (scal, attn_mine, attn_theirs, ff_mine, ff_theirs, *masters, *moments, *averages),
        name="update",
    )
    return (output[None], input_grad[None], *outs)


def solution(mesh):
    fine = Mesh(mesh.devices.reshape(4, 2, 4, 4), AXES)
    tokens = P(("y", "x"), ("z", "core"), None)
    rows = P(("z", "core", "y", "x"), None)
    return jax.shard_map(
        shards,
        mesh=fine,
        in_specs=(tokens, P(("y", "x"), ("z", "core")), tokens) + (rows,) * 24,
        out_specs=(tokens, tokens) + (rows,) * 32,
        check_vma=False,
    )
```

time: 1900 us -> 362 us (0.19); the launches traced: 1870 us -> 357 us
  blocking collectives: 587 us -> 0 us
  starting transfers between devices: 510 us -> 70.2 us
  waiting for transfers between devices: 420 us -> 132 us
  local copies, waits for them, and re-layouts: 232 us -> 29.3 us
  Pallas kernels: 0 us -> 77 us
  matrix products: 67.1 us -> 3.53 us
    unnamed x2 -> x0, blocking collectives: 526 us -> none
    unnamed x193 -> x0, starting transfers between devices: 510 us -> none
    all_gather x9 -> x1, waiting for transfers between devices: 408 us -> 50.1 us  [shards(): gathered = lax.all_gather(packed, ('z', 'y', 'x'), axis=0, tiled=False)]
    unnamed x427 -> x89, local copies, waits for them, and re-layouts: 226 us -> 15.1 us
    ppermute x0 -> x44, waiting for transfers between devices: none -> 82 us  [permute(): return lax.ppermute(value, AXES, pairs)]
    pallas_call x0 -> x10, Pallas kernels: none -> 77 us  [the longest x7 32.5 us: call(): pl.pallas_call(kernel, out_shape=out_shape, in_specs=specs, out_specs=jax...]
    ppermute x0 -> x44, starting transfers between devices: none -> 70.1 us  [permute(): return lax.ppermute(value, AXES, pairs)]
    dot_general x27 -> x2, matrix products: 67.1 us -> 3.53 us  [the longest x1 1.77 us: shards(): jnp.dot(x_all[:, HALF:], e2, preferred_element_type=F32)]
  transfers between devices with their start and end apart: 203 -> 45, of which waited for: 11 -> 23; matrix products, arithmetic and copies ran while one was open for 40% -> 12% of each run, Pallas kernels for 0% -> 13%
where the time goes in v1:
time: 362 us; the launch traced here: 357 us
  waiting for transfers between devices  132 us (36%)
  Pallas kernels  77 us (21%)
  starting transfers between devices  70.2 us (19%)
  other arithmetic  29.6 us (8%)
  local copies, waits for them, and re-layouts  29.3 us (8%)
  between operations  15.5 us (4%)
    ppermute x44, waiting for transfers between devices, permute(): return lax.ppermute(value, AXES, pairs)  82 us
    ppermute x44, starting transfers between devices, permute(): return lax.ppermute(value, AXES, pairs)  70.1 us
    all_gather x1, waiting for transfers between devices, shards(): gathered = lax.all_gather(packed, ('z', 'y', 'x'), axis=0, tiled=False)  50.1 us
    pallas_call x7, Pallas kernels, call(): pl.pallas_call(kernel, out_shape=out_shape, in_specs=specs, out_specs=jax...  32.5 us
    pallas_call x1, Pallas kernels, shards(): pl.pallas_call(ffn_kernel, out_shape=ffn_out, grid=(4,), in_specs=[scalar...  22.2 us
    unnamed x89, local copies, waits for them, and re-layouts  15.1 us
    pallas_call x1, Pallas kernels, shards(): pl.pallas_call(attn_forward_kernel, out_shape=forward_out, grid=(1,), in_...  13.8 us
    pallas_call x1, Pallas kernels, shards(): pl.pallas_call(attn_grads_kernel, out_shape=grads_out, grid=(1,), in_spec...  8.5 us
  transfers between devices with their start and end apart: 45, of which 23 were waited for; matrix products, arithmetic and copies ran while one was open for 12% of the time, Pallas kernels for 13%

profile of v1, /device:TPU:1, one launch (start us, length us, event | category | flops | bytes accessed | tf_op | source)
XLA Modules:
  0.0 357.1 jit_solution(8191347576212553981)
XLA Ops:
  20.3 3.3 collective-permute-start.1
  24.7 3.2 collective-permute-done
  28.3 5.3 %collective-permute-done.1 = bf16[144,768]{1,0:T(8,128)(2,1)S(1)} collective-permute-done((bf16[144,768]{1,0:T(8,128)(2,1)S(1)}, bf16[144,768]{1,0:T(8,128)(2,1)S(1)}, u32[]{:S(2)}, u32[]{:S(2)}) %collective-permute-start.1) | collective-permute-done | bytes 221216 | tf_op jit(solution)/shard_map/ppermute | solution.py:70
  43.3 6.3 %rev.3 = bf16[4,2,144,768]{3,0,2,1:T(4,128)(2,1)S(1)} reverse(bf16[4,2,144,768]{3,0,2,1:T(4,128)(2,1)S(1)} %maximum_select_fusion), dimensions={0} | reverse | bytes 3538944 | tf_op jit(solution)/shard_map/rev | solution.py:653
  49.6 3.2 fusion
  57.8 50.1 %all-gather.3.cloned.1.call-done = bf16[960,16,384]{2,1,0:T(8,128)(2,1)} async-done(((bf16[15,16,384]{2,1,0:T(8,128)(2,1)}), bf16[960,16,384]{2,1,0:T(8,128)(2,1)}) %all-gather.3.cloned.1.call-update) | async-done | bytes 11796496 | tf_op jit(solution)/shard_map/all_gather | solution.py:646
  111.0 2.6 fusion.20
  118.1 13.8 %attention_forward.1 = (bf16[1024,384]{1,0:T(8,128)(2,1)}, bf16[1024,384]{1,0:T(8,128)(2,1)}, bf16[1024,384]{1,0:T(8,128)(2,1)}, bf16[256,1024]{1,0:T(8,128)(2,1...) custom-call(s32[2]{0:T(128)} %pad_add_fusion.1.scal, ...), custom_call_target="tpu_custom_call" | custom-call | tf_op jit(solution)/shard_map/attention_forward/pallas_call | solution.py:688
  132.7 2.9 attention_output.1.part_a
  140.7 22.2 %feed_forward.1 = (f32[128,768]{1,0:T(8,128)}, f32[128,768]{1,0:T(8,128)}, f32[256,768]{1,0:T(8,128)}, f32[256,768]{1,0:T(8,128)}, f32[8,768]{1,0:T(8,128)}, /*i...) custom-call(s32[2]{0:T(128)} %pad_add_fusion.1.scal, ...), custom_call_target="tpu_custom_call" | custom-call | tf_op jit(solution)/shard_map/feed_forward/pallas_call | solution.py:723
  164.6 2.7 collective-permute-start.13
  169.7 3.7 %residual_backward.1 = (f32[2,128,768]{2,1,0:T(8,128)}, bf16[256,768]{1,0:T(8,128)(2,1)}, bf16[256,384]{1,0:T(8,128)(2,1)}) custom-call(s32[2]{0:T(128)} %pad_add_fusion.1.scal, f32[256,768]{1,0:T(8,128)} %get-tuple-element.121.resid, f32[256,768]{1,0:T(8,128)} %get-tuple-element.122.dh2_a, f32[256,768]{1,0:T(8,128)} %copy-done.7, ...), custom_call_target="tpu_custom_call" | custom-call | tf_op jit(solution)/shard_map/residual_backward/pallas_call | solution.py:590
  173.8 14.3 %collective-permute-done.12.o1 = bf16[256,512]{1,0:T(8,128)(2,1)S(1)} collective-permute-done((bf16[256,512]{1,0:T(8,128)(2,1)S(1)}, bf16[256,512]{1,0:T(8,128)(2,1)S(1)}, u32[]{:S(2)}, u32[]{:S(2)}) %collective-permute-start.12) | collective-permute-done | bytes 262176 | tf_op jit(solution)/shard_map/ppermute | solution.py:70
  188.1 3.6 %collective-permute-start.15 = (bf16[256,512]{1,0:T(8,128)(2,1)S(1)}, bf16[256,512]{1,0:T(8,128)(2,1)S(1)}, u32[]{:S(2)}, u32[]{:S(2)}) collective-permute-start(bf16[256,512]{1,0:T(8,128)(2,1)S(1)} %copy-done), channel_id=1, source_target_pairs={{0,16},{1,17},{2,18},{3,19},{4,20},{5,21},{6,22},{7,23},{8,24},{9,... | collective-permute-start | bytes 786440 | tf_op jit(solution)/shard_map/ppermute | solution.py:70
  196.7 5.4 %attention_query_gradient.1.dq = bf16[256,384]{1,0:T(8,128)(2,1)} custom-call(s32[2]{0:T(128)} %pad_add_fusion.1.scal, bf16[6,256,1024]{2,1,0:T(8,128)(2,1)} %get-tuple-element.118.probs, bf16[256,384]{1,0:T(8,128)(2,1)} %get-tuple-element.123.do.do0, bf16[256,512]{1,0:T(8,128)(2,1)} %get-tuple-element.119.o.o0.o_mine, ...), custom_call_target="tpu_custom_call" | custom-call | tf_op jit(solution)/shard_map/attention_query_gradient/pallas_call | solution.py:590
  203.7 11.7 %attention_key_gradient.1 = (bf16[256,384]{1,0:T(8,128)(2,1)}, bf16[256,384]{1,0:T(8,128)(2,1)}) custom-call(s32[2]{0:T(128)} %pad_add_fusion.1.scal, bf16[1024,384]{1,0:T(8,128)(2,1)} %get-tuple-element.126.q_all, bf16[1024,384]{1,0:T(8,128)(2,1)} %get-tuple-element.124.k_all, bf16[1024,384]{1,0:T(8,128)(2,1)} %get-tuple-element.125.v_all, ...), custom_call_target="tpu_custom_call" | custom-call | tf_op jit(solution)/shard_map/attention_key_gradient/pallas_call | solution.py:590
  216.1 8.5 %attention_weight_gradients.1 = (f32[128,1024]{1,0:T(8,128)}, f32[128,1024]{1,0:T(8,128)}, bf16[32,16,512]{2,1,0:T(8,128)(2,1)}, bf16[32,16,512]{2,1,0:T(8,128)(...) custom-call(s32[2]{0:T(128)} %pad_add_fusion.1.scal, ...), custom_call_target="tpu_custom_call" | custom-call | tf_op jit(solution)/shard_map/attention_weight_gradients/pallas_call | solution.py:782
  226.7 5.3 %collective-permute-start.17 = (f32[128,768]{1,0:T(8,128)}, f32[128,768]{1,0:T(8,128)S(1)}, u32[]{:S(2)}, u32[]{:S(2)}) collective-permute-start(f32[128,768]{1,0:T(8,128)} %get-tuple-element.137), channel_id=1, source_target_pairs={{0,16},{1,17},{2,18},{3,19},{4,20},{5,21},{6,22},{7,23},{8,24},{9,... | collective-permute-start | bytes 1179656 | tf_op jit(solution)/shard_map/ppermute | solution.py:70
  234.2 16.5 %collective-permute-done.21 = bf16[32,16,512]{2,1,0:T(8,128)(2,1)S(1)} collective-permute-done((bf16[32,16,512]{2,1,0:T(8,128)(2,1)}, bf16[32,16,512]{2,1,0:T(8,128)(2,1)S(1)}, u32[]{:S(2)}, u32[]{:S(2)}) %collective-permute-start.21) | collective-permute-done | bytes 524320 | tf_op jit(solution)/shard_map/ppermute | solution.py:70
  250.7 7.5 %collective-permute-start.16 = (f32[128,1024]{1,0:T(8,128)}, f32[128,1024]{1,0:T(8,128)S(1)}, u32[]{:S(2)}, u32[]{:S(2)}) collective-permute-start(f32[128,1024]{1,0:T(8,128)} %get-tuple-element.133), channel_id=1, source_target_pairs={{0,16},{1,17},{2,18},{3,19},{4,20},{5,21},{6,22},{7,23},{8,24},{9,... | collective-permute-start | bytes 1572872 | tf_op jit(solution)/shard_map/ppermute | solution.py:70
  262.2 5.3 %collective-permute-done.38 = bf16[16,3,16,384]{3,2,1,0:T(8,128)(2,1)S(1)} collective-permute-done((bf16[16,3,16,384]{3,2,1,0:T(8,128)(2,1)S(1)}, bf16[16,3,16,384]{3,2,1,0:T(8,128)(2,1)S(1)}, u32[]{:S(2)}, u32[]{:S(2)}) %collective-permute-start.38) | collective-permute-done | bytes 589856 | tf_op jit(solution)/shard_map/ppermute | solution.py:70
  268.1 4.6 %collective-permute-done.25 = bf16[16,16,512]{2,1,0:T(8,128)(2,1)S(1)} collective-permute-done((bf16[16,16,512]{2,1,0:T(8,128)(2,1)S(1)}, bf16[16,16,512]{2,1,0:T(8,128)(2,1)S(1)}, u32[]{:S(2)}, u32[]{:S(2)}) %collective-permute-start.25) | collective-permute-done | bytes 262176 | tf_op jit(solution)/shard_map/ppermute | solution.py:70
  272.8 7.7 %collective-permute-done.20 = bf16[8,16,512]{2,1,0:T(8,128)(2,1)S(1)} collective-permute-done((bf16[8,16,512]{2,1,0:T(8,128)(2,1)S(1)}, bf16[8,16,512]{2,1,0:T(8,128)(2,1)S(1)}, u32[]{:S(2)}, u32[]{:S(2)}) %collective-permute-start.20) | collective-permute-done | bytes 131104 | tf_op jit(solution)/shard_map/ppermute | solution.py:70
  282.1 2.6 collective-permute-done.23
  286.2 2.3 collective-permute-done.26
  290.0 4.0 %collective-permute-done.39 = bf16[8,3,16,384]{3,2,1,0:T(8,128)(2,1)S(1)} collective-permute-done((bf16[8,3,16,384]{3,2,1,0:T(8,128)(2,1)S(1)}, bf16[8,3,16,384]{3,2,1,0:T(8,128)(2,1)S(1)}, u32[]{:S(2)}, u32[]{:S(2)}) %collective-permute-start.39) | collective-permute-done | bytes 294944 | tf_op jit(solution)/shard_map/ppermute | solution.py:70
  296.7 3.1 collective-permute-done.27
  307.0 4.3 %token_outputs.1 = (bf16[128,768]{1,0:T(8,128)(2,1)}, f32[128,768]{1,0:T(8,128)}) custom-call(s32[2]{0:T(128)} %pad_add_fusion.1.scal, bf16[1024,1024]{1,0:T(8,128)(2,1)} %pad_maximum_fusion.xp, f32[128,1024]{1,0:T(8,128)} %get-tuple-element.132.dh1_a, f32[128,1024]{1,0:T(8,128)} %copy-done.9, f32[8,1024]{1,0:T(8,128)} %get-tuple-element.134.g1, ...), custom_call_target="tpu_custom_call" | custom-call | tf_op jit(solution)/shard_map/token_outputs/pallas_call | solution.py:590
  316.5 2.8 collective-permute-done.41
  321.7 15.7 %collective-permute-start.30 = (f32[8,1536]{1,0:T(8,128)S(1)}, f32[8,1536]{1,0:T(8,128)S(1)}, u32[]{:S(2)}, u32[]{:S(2)}) collective-permute-start(f32[8,1536]{1,0:T(8,128)S(1)} %get-tuple-element.496), channel_id=1, source_target_pairs={{0,16},{1,17},{2,18},{3,19},{4,20},{5,21},{6,22},{7,23},{8,24},{9,... | collective-permute-start | bytes 147464 | tf_op jit(solution)/shard_map/ppermute | solution.py:70
  337.5 3.0 collective-permute-start.43
  342.1 2.6 update.1
  (245 shorter events, 91.6 us)
Async XLA Ops:
  7.2 100.7 %all-gather.3.cloned.1.call-start = ((), (), s32[]{:S(2)}) async-start(), calls=%async_computation | async-start | bytes 11980800 | tf_op jit(solution)/shard_map/all_gather | solution.py:646
  18.5 9.4 %collective-permute-start = (bf16[144,768]{1,0:T(8,128)(2,1)S(1)}, bf16[144,768]{1,0:T(8,128)(2,1)S(1)}, u32[]{:S(2)}, u32[]{:S(2)}) collective-permute-start(bf16[144,768]{1,0:T(8,128)(2,1)S(1)} %get-tuple-element.493), channel_id=1, source_target_pairs={{0,32},{1,33},{2,34},{3,35},{4,36},{5,37},{6,38},{7,39},{8,40},{9,... | collective-permute-start | bytes 663560 | tf_op jit(solution)/shard_map/ppermute | solution.py:70
  20.3 13.2 %collective-permute-start.1 = (bf16[144,768]{1,0:T(8,128)(2,1)S(1)}, bf16[144,768]{1,0:T(8,128)(2,1)S(1)}, u32[]{:S(2)}, u32[]{:S(2)}) collective-permute-start(bf16[144,768]{1,0:T(8,128)(2,1)S(1)} %get-tuple-element.493), channel_id=1, source_target_pairs={{0,64},{1,65},{2,66},{3,67},{4,68},{5,69},{6,70},{7,71},{8,72},{9,... | collective-permute-start | bytes 663560 | tf_op jit(solution)/shard_map/ppermute | solution.py:70
  23.6 10.3 %collective-permute-start.2 = (bf16[144,768]{1,0:T(8,128)(2,1)S(1)}, bf16[144,768]{1,0:T(8,128)(2,1)S(1)}, u32[]{:S(2)}, u32[]{:S(2)}) collective-permute-start(bf16[144,768]{1,0:T(8,128)(2,1)S(1)} %get-tuple-element.493), channel_id=1, source_target_pairs={{0,96},{1,97},{2,98},{3,99},{4,100},{5,101},{6,102},{7,103},{8,104... | collective-permute-start | bytes 663560 | tf_op jit(solution)/shard_map/ppermute | solution.py:70
  109.9 22.0 %collective-permute-start.5 = (bf16[32,16,384]{2,1,0:T(8,128)(2,1)}, bf16[32,16,384]{2,1,0:T(8,128)(2,1)S(1)}, u32[]{:S(2)}, u32[]{:S(2)}) collective-permute-start(bf16[32,16,384]{2,1,0:T(8,128)(2,1)} %get-tuple-element.490), channel_id=1, source_target_pairs={{0,16},{1,17},{2,18},{3,19},{4,20},{5,21},{6,22},{7,23},{8,24},{9,... | collective-permute-start | bytes 1179656 | tf_op jit(solution)/shard_map/ppermute | solution.py:70
  163.1 68.9 %collective-permute-start.37 = (bf16[32,3,16,384]{3,2,1,0:T(8,128)(2,1)}, bf16[32,3,16,384]{3,2,1,0:T(8,128)(2,1)}, u32[]{:S(2)}, u32[]{:S(2)}) collective-permute-start(bf16[32,3,16,384]{3,2,1,0:T(8,128)(2,1)} %get-tuple-element.151), channel_id=1, source_target_pairs={{0,96},{1,97},{2,98},{3,99},{4,100},{5,101},{6,102},{7,103},{8,104... | collective-permute-start | bytes 3538952 | tf_op jit(solution)/shard_map/ppermute | solution.py:70
  164.2 23.9 %collective-permute-start.12 = (bf16[256,512]{1,0:T(8,128)(2,1)S(1)}, bf16[256,512]{1,0:T(8,128)(2,1)S(1)}, u32[]{:S(2)}, u32[]{:S(2)}) collective-permute-start(bf16[256,512]{1,0:T(8,128)(2,1)S(1)} %copy-done), channel_id=1, source_target_pairs={{0,32},{1,33},{2,34},{3,35},{4,36},{5,37},{6,38},{7,39},{8,40},{9,... | collective-permute-start | bytes 786440 | tf_op jit(solution)/shard_map/ppermute | solution.py:70
  164.6 29.3 %collective-permute-start.13 = (bf16[256,512]{1,0:T(8,128)(2,1)S(1)}, bf16[256,512]{1,0:T(8,128)(2,1)S(1)}, u32[]{:S(2)}, u32[]{:S(2)}) collective-permute-start(bf16[256,512]{1,0:T(8,128)(2,1)S(1)} %copy-done), channel_id=1, source_target_pairs={{0,64},{1,65},{2,66},{3,67},{4,68},{5,69},{6,70},{7,71},{8,72},{9,... | collective-permute-start | bytes 786440 | tf_op jit(solution)/shard_map/ppermute | solution.py:70
  167.2 27.8 %collective-permute-start.14 = (bf16[256,512]{1,0:T(8,128)(2,1)S(1)}, bf16[256,512]{1,0:T(8,128)(2,1)S(1)}, u32[]{:S(2)}, u32[]{:S(2)}) collective-permute-start(bf16[256,512]{1,0:T(8,128)(2,1)S(1)} %copy-done), channel_id=1, source_target_pairs={{0,96},{1,97},{2,98},{3,99},{4,100},{5,101},{6,102},{7,103},{8,104... | collective-permute-start | bytes 786440 | tf_op jit(solution)/shard_map/ppermute | solution.py:70
  173.4 22.6 %collective-permute-start.10 = (bf16[256,384]{1,0:T(8,128)(2,1)}, bf16[256,384]{1,0:T(8,128)(2,1)S(1)}, u32[]{:S(2)}, u32[]{:S(2)}) collective-permute-start(bf16[256,384]{1,0:T(8,128)(2,1)} %get-tuple-element.123.do.do0), channel_id=1, source_target_pairs={{0,64},{1,65},{2,66},{3,67},{4,68},{5,69},{6,70},{7,71},{8,72},{9,... | collective-permute-start | bytes 589832 | tf_op jit(solution)/shard_map/ppermute | solution.py:70
  188.1 27.4 %collective-permute-start.15 = (bf16[256,512]{1,0:T(8,128)(2,1)S(1)}, bf16[256,512]{1,0:T(8,128)(2,1)S(1)}, u32[]{:S(2)}, u32[]{:S(2)}) collective-permute-start(bf16[256,512]{1,0:T(8,128)(2,1)S(1)} %copy-done), channel_id=1, source_target_pairs={{0,16},{1,17},{2,18},{3,19},{4,20},{5,21},{6,22},{7,23},{8,24},{9,... | collective-permute-start | bytes 786440 | tf_op jit(solution)/shard_map/ppermute | solution.py:70
  193.9 64.8 %collective-permute-start.31 = (bf16[32,4,16,384]{3,2,1,0:T(8,128)(2,1)}, bf16[32,4,16,384]{3,2,1,0:T(8,128)(2,1)S(1)}, u32[]{:S(2)}, u32[]{:S(2)}) collective-permute-start(bf16[32,4,16,384]{3,2,1,0:T(8,128)(2,1)} %get-tuple-element.147), channel_id=1, source_target_pairs={{0,3},{1,2},{2,1},{3,0},{4,7},{5,6},{6,5},{7,4},{8,11},{9,10},{10,... | collective-permute-start | bytes 4718600 | tf_op jit(solution)/shard_map/ppermute | solution.py:70
  195.1 7.1 %collective-permute-start.11 = (bf16[256,384]{1,0:T(8,128)(2,1)}, bf16[256,384]{1,0:T(8,128)(2,1)S(1)}, u32[]{:S(2)}, u32[]{:S(2)}) collective-permute-start(bf16[256,384]{1,0:T(8,128)(2,1)} %get-tuple-element.123.do.do0), channel_id=1, source_target_pairs={{0,96},{1,97},{2,98},{3,99},{4,100},{5,101},{6,102},{7,103},{8,104... | collective-permute-start | bytes 589832 | tf_op jit(solution)/shard_map/ppermute | solution.py:70
  196.0 7.0 %collective-permute-start.9 = (bf16[256,384]{1,0:T(8,128)(2,1)}, bf16[256,384]{1,0:T(8,128)(2,1)S(1)}, u32[]{:S(2)}, u32[]{:S(2)}) collective-permute-start(bf16[256,384]{1,0:T(8,128)(2,1)} %get-tuple-element.123.do.do0), channel_id=1, source_target_pairs={{0,32},{1,33},{2,34},{3,35},{4,36},{5,37},{6,38},{7,39},{8,40},{9,... | collective-permute-start | bytes 589832 | tf_op jit(solution)/shard_map/ppermute | solution.py:70
  224.6 9.2 %collective-permute-start.18 = (bf16[32,16,512]{2,1,0:T(8,128)(2,1)}, bf16[32,16,512]{2,1,0:T(8,128)(2,1)S(1)}, u32[]{:S(2)}, u32[]{:S(2)}) collective-permute-start(bf16[32,16,512]{2,1,0:T(8,128)(2,1)} %get-tuple-element.141), channel_id=1, source_target_pairs={{0,3},{1,2},{2,1},{3,0},{4,7},{5,6},{6,5},{7,4},{8,11},{9,10},{10,... | collective-permute-start | bytes 1572872 | tf_op jit(solution)/shard_map/ppermute | solution.py:70
  224.8 35.5 %collective-permute-start.34 = (bf16[32,4,16,384]{3,2,1,0:T(8,128)(2,1)}, bf16[32,4,16,384]{3,2,1,0:T(8,128)(2,1)S(1)}, u32[]{:S(2)}, u32[]{:S(2)}) collective-permute-start(bf16[32,4,16,384]{3,2,1,0:T(8,128)(2,1)} %get-tuple-element.149), channel_id=1, source_target_pairs={{0,12},{1,13},{2,14},{3,15},{4,8},{5,9},{6,10},{7,11},{8,4},{9,5},... | collective-permute-start | bytes 4718600 | tf_op jit(solution)/shard_map/ppermute | solution.py:70
  226.7 79.3 %collective-permute-start.17 = (f32[128,768]{1,0:T(8,128)}, f32[128,768]{1,0:T(8,128)S(1)}, u32[]{:S(2)}, u32[]{:S(2)}) collective-permute-start(f32[128,768]{1,0:T(8,128)} %get-tuple-element.137), channel_id=1, source_target_pairs={{0,16},{1,17},{2,18},{3,19},{4,20},{5,21},{6,22},{7,23},{8,24},{9,... | collective-permute-start | bytes 1179656 | tf_op jit(solution)/shard_map/ppermute | solution.py:70
  232.0 18.6 %collective-permute-start.21 = (bf16[32,16,512]{2,1,0:T(8,128)(2,1)}, bf16[32,16,512]{2,1,0:T(8,128)(2,1)S(1)}, u32[]{:S(2)}, u32[]{:S(2)}) collective-permute-start(bf16[32,16,512]{2,1,0:T(8,128)(2,1)} %get-tuple-element.143), channel_id=1, source_target_pairs={{0,12},{1,13},{2,14},{3,15},{4,8},{5,9},{6,10},{7,11},{8,4},{9,5},... | collective-permute-start | bytes 1572872 | tf_op jit(solution)/shard_map/ppermute | solution.py:70
  233.8 24.6 %collective-permute-start.24 = (bf16[32,16,512]{2,1,0:T(8,128)(2,1)S(1)}, bf16[32,16,512]{2,1,0:T(8,128)(2,1)S(1)}, u32[]{:S(2)}, u32[]{:S(2)}) collective-permute-start(bf16[32,16,512]{2,1,0:T(8,128)(2,1)S(1)} %copy-done.40), channel_id=1, source_target_pairs={{0,96},{1,97},{2,98},{3,99},{4,100},{5,101},{6,102},{7,103},{8,104... | collective-permute-start | bytes 1572872 | tf_op jit(solution)/shard_map/ppermute | solution.py:70
  250.7 55.4 %collective-permute-start.16 = (f32[128,1024]{1,0:T(8,128)}, f32[128,1024]{1,0:T(8,128)S(1)}, u32[]{:S(2)}, u32[]{:S(2)}) collective-permute-start(f32[128,1024]{1,0:T(8,128)} %get-tuple-element.133), channel_id=1, source_target_pairs={{0,16},{1,17},{2,18},{3,19},{4,20},{5,21},{6,22},{7,23},{8,24},{9,... | collective-permute-start | bytes 1572872 | tf_op jit(solution)/shard_map/ppermute | solution.py:70
  258.4 9.1 %collective-permute-start.38 = (bf16[16,3,16,384]{3,2,1,0:T(8,128)(2,1)S(1)}, bf16[16,3,16,384]{3,2,1,0:T(8,128)(2,1)S(1)}, u32[]{:S(2)}, u32[]{:S(2)}) collective-permute-start(bf16[16,3,16,384]{3,2,1,0:T(8,128)(2,1)S(1)} %slice.228), channel_id=1, source_target_pairs={{0,3},{1,2},{2,1},{3,0},{4,7},{5,6},{6,5},{7,4},{8,11},{9,10},{10,... | collective-permute-start | bytes 1769480 | tf_op jit(solution)/shard_map/ppermute | solution.py:70
  258.7 8.9 %collective-permute-start.19 = (bf16[16,16,512]{2,1,0:T(8,128)(2,1)S(1)}, bf16[16,16,512]{2,1,0:T(8,128)(2,1)S(1)}, u32[]{:S(2)}, u32[]{:S(2)}) collective-permute-start(bf16[16,16,512]{2,1,0:T(8,128)(2,1)S(1)} %slice.202), channel_id=1, source_target_pairs={{0,12},{1,13},{2,14},{3,15},{4,8},{5,9},{6,10},{7,11},{8,4},{9,5},... | collective-permute-start | bytes 786440 | tf_op jit(solution)/shard_map/ppermute | solution.py:70
  260.3 7.7 %collective-permute-start.22 = (bf16[16,16,512]{2,1,0:T(8,128)(2,1)S(1)}, bf16[16,16,512]{2,1,0:T(8,128)(2,1)S(1)}, u32[]{:S(2)}, u32[]{:S(2)}) collective-permute-start(bf16[16,16,512]{2,1,0:T(8,128)(2,1)S(1)} %slice.206), channel_id=1, source_target_pairs={{0,96},{1,97},{2,98},{3,99},{4,100},{5,101},{6,102},{7,103},{8,104... | collective-permute-start | bytes 786440 | tf_op jit(solution)/shard_map/ppermute | solution.py:70
  267.7 27.6 %collective-permute-start.32 = (bf16[16,4,16,384]{3,2,1,0:T(8,128)(2,1)S(1)}, bf16[16,4,16,384]{3,2,1,0:T(8,128)(2,1)S(1)}, u32[]{:S(2)}, u32[]{:S(2)}) collective-permute-start(bf16[16,4,16,384]{3,2,1,0:T(8,128)(2,1)S(1)} %slice.220), channel_id=1, source_target_pairs={{0,12},{1,13},{2,14},{3,15},{4,8},{5,9},{6,10},{7,11},{8,4},{9,5},... | collective-permute-start | bytes 2359304 | tf_op jit(solution)/shard_map/ppermute | solution.py:70
  267.9 27.7 %collective-permute-start.35 = (bf16[16,4,16,384]{3,2,1,0:T(8,128)(2,1)S(1)}, bf16[16,4,16,384]{3,2,1,0:T(8,128)(2,1)S(1)}, u32[]{:S(2)}, u32[]{:S(2)}) collective-permute-start(bf16[16,4,16,384]{3,2,1,0:T(8,128)(2,1)S(1)} %slice.224), channel_id=1, source_target_pairs={{0,96},{1,97},{2,98},{3,99},{4,100},{5,101},{6,102},{7,103},{8,104... | collective-permute-start | bytes 2359304 | tf_op jit(solution)/shard_map/ppermute | solution.py:70
  272.7 7.8 %collective-permute-start.20 = (bf16[8,16,512]{2,1,0:T(8,128)(2,1)S(1)}, bf16[8,16,512]{2,1,0:T(8,128)(2,1)S(1)}, u32[]{:S(2)}, u32[]{:S(2)}) collective-permute-start(bf16[8,16,512]{2,1,0:T(8,128)(2,1)S(1)} %slice.204), channel_id=1, source_target_pairs={{0,96},{1,97},{2,98},{3,99},{4,100},{5,101},{6,102},{7,103},{8,104... | collective-permute-start | bytes 393224 | tf_op jit(solution)/shard_map/ppermute | solution.py:70
  295.5 6.7 %collective-permute-start.33 = (bf16[8,4,16,384]{3,2,1,0:T(8,128)(2,1)S(1)}, bf16[8,4,16,384]{3,2,1,0:T(8,128)(2,1)S(1)}, u32[]{:S(2)}, u32[]{:S(2)}) collective-permute-start(bf16[8,4,16,384]{3,2,1,0:T(8,128)(2,1)S(1)} %slice.222), channel_id=1, source_target_pairs={{0,96},{1,97},{2,98},{3,99},{4,100},{5,101},{6,102},{7,103},{8,104... | collective-permute-start | bytes 1179656 | tf_op jit(solution)/shard_map/ppermute | solution.py:70
  295.9 6.7 %collective-permute-start.36 = (bf16[8,4,16,384]{3,2,1,0:T(8,128)(2,1)S(1)}, bf16[8,4,16,384]{3,2,1,0:T(8,128)(2,1)S(1)}, u32[]{:S(2)}, u32[]{:S(2)}) collective-permute-start(bf16[8,4,16,384]{3,2,1,0:T(8,128)(2,1)S(1)} %slice.226), channel_id=1, source_target_pairs={{0,3},{1,2},{2,1},{3,0},{4,7},{5,6},{6,5},{7,4},{8,11},{9,10},{10,... | collective-permute-start | bytes 1179656 | tf_op jit(solution)/shard_map/ppermute | solution.py:70
  299.9 11.3 %collective-permute-start.28 = (bf16[2,16,1536]{2,1,0:T(8,128)(2,1)S(1)}, bf16[2,16,1536]{2,1,0:T(8,128)(2,1)S(1)}, u32[]{:S(2)}, u32[]{:S(2)}) collective-permute-start(bf16[2,16,1536]{2,1,0:T(8,128)(2,1)S(1)} %slice.216), channel_id=1, source_target_pairs={{0,4},{1,5},{2,6},{3,7},{4,0},{5,1},{6,2},{7,3},{8,12},{9,13},{10,... | collective-permute-start | bytes 294920 | tf_op jit(solution)/shard_map/ppermute | solution.py:70
  303.0 9.5 %collective-permute-start.40 = (bf16[4,11,16,384]{3,2,1,0:T(8,128)(2,1)S(1)}, bf16[4,11,16,384]{3,2,1,0:T(8,128)(2,1)S(1)}, u32[]{:S(2)}, u32[]{:S(2)}) collective-permute-start(bf16[4,11,16,384]{3,2,1,0:T(8,128)(2,1)S(1)} %slice.232), channel_id=1, source_target_pairs={{0,1},{1,0},{2,3},{3,2},{4,5},{5,4},{6,7},{7,6},{8,9},{9,8},{10,11... | collective-permute-start | bytes 1622024 | tf_op jit(solution)/shard_map/ppermute | solution.py:70
  319.4 18.0 %collective-permute-start.42 = (bf16[1,11,16,384]{3,2,1,0:T(8,128)(2,1)S(1)}, bf16[1,11,16,384]{3,2,1,0:T(8,128)(2,1)S(1)}, u32[]{:S(2)}, u32[]{:S(2)}) collective-permute-start(bf16[1,11,16,384]{3,2,1,0:T(8,128)(2,1)S(1)} %slice.236), channel_id=1, source_target_pairs={{0,32},{1,33},{2,34},{3,35},{4,36},{5,37},{6,38},{7,39},{8,40},{9,... | collective-permute-start | bytes 405512 | tf_op jit(solution)/shard_map/ppermute | solution.py:70
  321.7 19.5 %collective-permute-start.30 = (f32[8,1536]{1,0:T(8,128)S(1)}, f32[8,1536]{1,0:T(8,128)S(1)}, u32[]{:S(2)}, u32[]{:S(2)}) collective-permute-start(f32[8,1536]{1,0:T(8,128)S(1)} %get-tuple-element.496), channel_id=1, source_target_pairs={{0,16},{1,17},{2,18},{3,19},{4,20},{5,21},{6,22},{7,23},{8,24},{9,... | collective-permute-start | bytes 147464 | tf_op jit(solution)/shard_map/ppermute | solution.py:70
  (54 other events, 269.9 us)
Sparse Core Ops, SparseCore 0:
  17.0 90.7 all-gather.2
